TPU v7x, 512 devices: a whole 4x4x16 slice. The times are simulated.
512 devices in a mesh: gx: 8 (over x, z_hi), gy: 8 (over z_lo), gz: 8 (over y, core).
Axes of the slice: x: 4, y: 4, z: 16 (z_hi: 2, z_lo: 8; z = z_hi * 8 + z_lo), core: 2. Of those that a mesh axis runs over, the one named last changes fastest.
Arguments:
- positions: float32 [3, 32, 32, 16, 128], P(None, 'gx', 'gy', 'gz'), as said below
- volume: float32 [32, 32, 16, 128], P('gx', 'gy', 'gz'), may hold values from 0.5 to 2
- displacement: float32 [3, 32, 32, 16, 128], P(None, 'gx', 'gy', 'gz'), may hold values from -0.12 to 0.12
- velocity: float32 [3, 32, 32, 16, 128], P(None, 'gx', 'gy', 'gz'), may hold values from -1 to 1
- acceleration: float32 [3, 32, 32, 16, 128], P(None, 'gx', 'gy', 'gz'), may hold values from -4 to 4
- tile_own: int32 [8, 8, 8, 40], P('gx', 'gy', 'gz'), may hold values from 29 to 114, as said below
- tile_partner: int32 [8, 8, 8, 40], P('gx', 'gy', 'gz'), may hold values from 0 to 143, as said below
- tile_count: int32 [8, 8, 8], P('gx', 'gy', 'gz'), may hold values from 30 to 40, as said below
- family_bits: int32 [8, 8, 8, 40, 16, 128], P('gx', 'gy', 'gz'), may hold values from 0 to 255, as said below
- broken_bits: int32 [8, 8, 8, 40, 16, 128], P('gx', 'gy', 'gz'), may hold values from 0 to 255, as said below
Outputs:
- final_displacement: float32 [3, 32, 32, 16, 128], P(None, 'gx', 'gy', 'gz')
- final_velocity: float32 [3, 32, 32, 16, 128], P(None, 'gx', 'gy', 'gz')
- final_acceleration: float32 [3, 32, 32, 16, 128], P(None, 'gx', 'gy', 'gz')
Inputs may be any that keep to these rules, and one draw needn't show every extreme that they name: `tile_own`: each entry names an interior block of the device's padded grid of (6) x (6) x (4) blocks, numbered row-major. `tile_partner`: each entry is tile_own of the same slot moved by one of the 27 block offsets (dx, dy, dz) with dx, dy, dz in -1, 0, 1. `tile_count`: each device uses 40 or 30 slots, the first ones; both counts occur. `family_bits`: eight bond bits a word, bit k of word w of row a for partner point 8 w + k. `broken_bits`: eight bond bits a word, laid out as family_bits. `positions`: each block holds a 4 x 4 x 8 lattice of points of spacing 1, block (i, j, k) starting at (4 i, 4 j, 8 k); every coordinate of a point lies within 0.2 of its lattice site's, 0.5 past the lower corner.
All inputs are finite; a program needn't handle non-finite values.
Results may differ from a plain program's by a relative error of at most 0.0003.
Values sent between devices are 32-bit elements; how exact they have to be, the bound alone decides.
A program may use at most 64 MiB of HBM per device.

v0:
```python
import jax
import jax.numpy as jnp
from jax import lax
from jax.sharding import PartitionSpec as P

GROUP = 8
STEPS = 2


K_BULK = 8000.0
MU_SHEAR = 600.0
VOLUME_FLOOR = 2000.0
TIME_DELTA = 0.05


def shifted(value, axis, steps):
    count = lax.axis_size(axis)
    leading, last = (max(0, -steps), min(count, count - steps))
    return lax.ppermute(value, axis, [(source, source + steps) for source in range(leading, last)])


def with_halo(array, sides, width):
    for axis, dim in sides:
        peers, length = (lax.axis_size(axis), array.shape[dim])
        up = [(i, (i + 1) % peers) for i in range(peers - 1)]
        down = [(j, i) for i, j in up]
        last = lax.slice_in_dim(array, length - width, length, axis=dim)
        leading = lax.slice_in_dim(array, 0, width, axis=dim)
        before = lax.ppermute(last, axis, up)
        after = lax.ppermute(leading, axis, down)
        array = jnp.concatenate([before, array, after], axis=dim)
    return array


def bond_bits(packed):
    by_rows = jnp.swapaxes(packed, 1, 2)
    spread = jnp.repeat(by_rows, 8, axis=2)
    bit_place = jnp.arange(spread.shape[2], dtype=jnp.int32) % 8
    return jnp.bitwise_and(jnp.right_shift(spread, bit_place), 1)


def bond_geometry(static_pad, disp_pad, own_block, partner_block, family, broken, live_slot):
    near_data = jnp.take(static_pad, own_block, axis=1)
    far_data = jnp.take(static_pad, partner_block, axis=1)
    near_disp = jnp.take(disp_pad, own_block, axis=1)
    far_disp = jnp.take(disp_pad, partner_block, axis=1)
    offset = far_data[:3, :, None, :] - near_data[:3, :, :, None]
    stretch = offset + far_disp[:, :, None, :] - near_disp[:, :, :, None]
    point_index = jnp.arange(offset.shape[3], dtype=jnp.int32)
    upper_half = point_index[None, :] > point_index[:, None]
    self_tile = (own_block == partner_block)[:, None, None]
    alive = bond_bits(family) * (1 - bond_bits(broken)) > 0
    alive = alive & (upper_half[None] | jnp.logical_not(self_tile)) & live_slot[:, None, None]
    weight = alive.astype(jnp.float32)
    rest_length = jnp.sqrt(jnp.where(alive, jnp.sum(offset * offset, axis=0), 1.0))
    bond_length = jnp.sqrt(jnp.where(alive, jnp.sum(stretch * stretch, axis=0), 1.0))
    return (
        weight,
        rest_length,
        bond_length - rest_length,
        stretch / bond_length,
        near_data[3],
        far_data[3],
    )


def dilatation_terms(geometry, extra_data, own_block, partner_block):
    weight, rest_length, extension, unit_direction, near_volume, far_volume = geometry
    stretch_term = weight * rest_length * extension
    square = weight * rest_length * rest_length
    near_terms = jnp.stack(
        [
            jnp.sum(stretch_term * far_volume[:, None, :], axis=2),
            jnp.sum(square * far_volume[:, None, :], axis=2),
        ]
    )
    far_terms = jnp.stack(
        [
            jnp.sum(stretch_term * near_volume[:, :, None], axis=1),
            jnp.sum(square * near_volume[:, :, None], axis=1),
        ]
    )
    return (near_terms, far_terms)


def force_terms(geometry, coef_pad, own_block, partner_block):
    weight, rest_length, extension, unit_direction, near_volume, far_volume = geometry
    near_coef = jnp.take(coef_pad, own_block, axis=1)
    far_coef = jnp.take(coef_pad, partner_block, axis=1)
    magnitude = weight * (
        rest_length * (near_coef[0][:, :, None] + far_coef[0][:, None, :])
        + extension * (near_coef[1][:, :, None] + far_coef[1][:, None, :])
    )
    bond_force = magnitude[None] * unit_direction
    near_terms = jnp.sum(bond_force * far_volume[None, :, None, :], axis=3)
    far_terms = -jnp.sum(bond_force * near_volume[None, :, :, None], axis=2)
    return (near_terms, far_terms)


def tile_pass(
    kernel,
    channels,
    static_pad,
    disp_pad,
    extra_data,
    own_list,
    partner_list,
    family,
    broken,
    live_count,
):
    running = jnp.zeros((channels, static_pad.shape[1], static_pad.shape[2]), jnp.float32)

    def group_step(group_index, running):
        first_slot = (group_index * GROUP).astype(jnp.int32)
        own_block = lax.dynamic_slice_in_dim(own_list, first_slot, GROUP)
        partner_block = lax.dynamic_slice_in_dim(partner_list, first_slot, GROUP)
        family_group = lax.dynamic_slice_in_dim(family, first_slot, GROUP)
        broken_group = lax.dynamic_slice_in_dim(broken, first_slot, GROUP)
        slot_index = first_slot + jnp.arange(GROUP, dtype=jnp.int32)
        geometry = bond_geometry(
            static_pad,
            disp_pad,
            own_block,
            partner_block,
            family_group,
            broken_group,
            slot_index < live_count,
        )
        near_terms, far_terms = kernel(geometry, extra_data, own_block, partner_block)
        running = running.at[:, own_block].add(near_terms)
        return running.at[:, partner_block].add(far_terms)

    groups = (live_count + GROUP - 1) // GROUP
    return lax.fori_loop(jnp.int32(0), groups, group_step, running)


def material_coefs(volume_sums):
    floored = jnp.maximum(volume_sums[1], VOLUME_FLOOR)
    dilatation = 3.0 * volume_sums[0] / floored
    return jnp.stack(
        [dilatation * (3.0 * K_BULK - 5.0 * MU_SHEAR) / floored, 15.0 * MU_SHEAR / floored]
    )


def flat_blocks(values_in):
    return values_in.reshape(values_in.shape[0], -1, values_in.shape[-1])


def send_x(ghost_slab, direction):
    return shifted(ghost_slab, "gx", direction)


def send_y(ghost_slab, direction):
    return shifted(ghost_slab, "gy", direction)


def send_z(ghost_slab, direction):
    return shifted(ghost_slab, "gz", direction)


def fold_axis(partial_value, dim, sender):
    size_here = partial_value.shape[dim]
    for direction, source, target in ((-1, 0, size_here - 2), (1, size_here - 1, 1)):
        ghost_slab = lax.slice_in_dim(partial_value, source, source + 1, axis=dim)
        arrived = sender(ghost_slab, direction)
        target_slab = lax.slice_in_dim(partial_value, target, target + 1, axis=dim) + arrived
        partial_value = lax.dynamic_update_slice_in_dim(
            partial_value, target_slab, target, axis=dim
        )
    return lax.slice_in_dim(partial_value, 1, size_here - 1, axis=dim)


def fold_ghosts(partial_value, interior_shape):
    partial_value = partial_value.reshape(
        partial_value.shape[0],
        interior_shape[1] + 2,
        interior_shape[2] + 2,
        interior_shape[3] + 2,
        interior_shape[4],
    )
    partial_value = fold_axis(partial_value, 1, send_x)
    partial_value = fold_axis(partial_value, 2, send_y)
    partial_value = fold_axis(partial_value, 3, send_z)
    return partial_value


def per_device(
    positions,
    volume,
    displacement,
    velocity,
    acceleration,
    tile_own,
    tile_partner,
    tile_count,
    family_bits,
    broken_bits,
):
    tile_slots = tile_own.shape[-1]
    own_list = tile_own.reshape(tile_slots)
    partner_list = tile_partner.reshape(tile_slots)
    live_count = tile_count.reshape(())
    family = family_bits.reshape(tile_slots, family_bits.shape[-2], family_bits.shape[-1])
    broken = broken_bits.reshape(tile_slots, broken_bits.shape[-2], broken_bits.shape[-1])
    static = jnp.concatenate([positions, volume[None]], axis=0)
    half_vel = velocity + 0.5 * TIME_DELTA * acceleration
    displacement = displacement + TIME_DELTA * half_vel
    static_pad = flat_blocks(with_halo(static, (("gx", 1), ("gy", 2), ("gz", 3)), 1))
    disp_pad = flat_blocks(with_halo(displacement, (("gx", 1), ("gy", 2), ("gz", 3)), 1))
    for time_step in range(STEPS):
        if time_step > 0:
            half_vel = velocity + 0.5 * TIME_DELTA * acceleration
            displacement = displacement + TIME_DELTA * half_vel
            disp_pad = flat_blocks(with_halo(displacement, (("gx", 1), ("gy", 2), ("gz", 3)), 1))
        volume_sums = fold_ghosts(
            tile_pass(
                dilatation_terms,
                2,
                static_pad,
                disp_pad,
                static_pad,
                own_list,
                partner_list,
                family,
                broken,
                live_count,
            ),
            displacement.shape,
        )
        bond_coefs = material_coefs(volume_sums)
        coef_pad = flat_blocks(with_halo(bond_coefs, (("gx", 1), ("gy", 2), ("gz", 3)), 1))
        acceleration = fold_ghosts(
            tile_pass(
                force_terms,
                3,
                static_pad,
                disp_pad,
                coef_pad,
                own_list,
                partner_list,
                family,
                broken,
                live_count,
            ),
            displacement.shape,
        )
        velocity = half_vel + 0.5 * TIME_DELTA * acceleration
    return (displacement, velocity, acceleration)


def solution(mesh):
    in_specs = (
        P(None, "gx", "gy", "gz", None),
        P("gx", "gy", "gz", None),
        P(None, "gx", "gy", "gz", None),
        P(None, "gx", "gy", "gz", None),
        P(None, "gx", "gy", "gz", None),
        P("gx", "gy", "gz", None),
        P("gx", "gy", "gz", None),
        P("gx", "gy", "gz"),
        P("gx", "gy", "gz", None, None, None),
        P("gx", "gy", "gz", None, None, None),
    )
    out_specs = (
        P(None, "gx", "gy", "gz", None),
        P(None, "gx", "gy", "gz", None),
        P(None, "gx", "gy", "gz", None),
    )
    return jax.shard_map(
        per_device, mesh=mesh, in_specs=in_specs, out_specs=out_specs, check_vma=False
    )
```

profile of v0, /device:TPU:392, one launch (start us, length us, event | category | flops | bytes accessed | tf_op | source)
XLA Modules:
  0.0 584.1 jit_solution(16373525324118412953)
XLA Ops:
  6.2 10.0 %collective-permute-start.7 = (f32[3,1,4,2,128]{4,3,2,1,0:T(2,128)S(1)}, f32[3,1,4,2,128]{4,3,2,1,0:T(2,128)S(1)}, u32[]{:S(2)}, u32[]{:S(2)}) collective-permute-start(f32[3,1,4,2,128]{4,3,2,1,0:T(2,128)S(1)} %get-tuple-element.903), channel_id=1, source_target_pairs={{64,0},{128,64},{192,128},{256,192},{320,256},{384,320},{448,384},... | collective-permute-start | bytes 36872 | tf_op jit(solution)/shard_map/ppermute | solution.py:30
  16.9 5.5 collective-permute-start
  22.4 9.1 %collective-permute-start.1 = (f32[4,1,4,2,128]{4,3,2,1,0:T(2,128)S(1)}, f32[4,1,4,2,128]{4,3,2,1,0:T(2,128)S(1)}, u32[]{:S(2)}, u32[]{:S(2)}) collective-permute-start(f32[4,1,4,2,128]{4,3,2,1,0:T(2,128)S(1)} %get-tuple-element.895), channel_id=1, source_target_pairs={{64,0},{128,64},{192,128},{256,192},{320,256},{384,320},{448,384},... | collective-permute-start | bytes 49160 | tf_op jit(solution)/shard_map/ppermute | solution.py:30
  61.1 39.8 %while.48 = (s32[]{:T(128)}, f32[2,144,128]{2,0,1:T(2,128)S(1)}, s32[]{:T(128)}, s32[40]{0:T(128)S(1)}, s32[40,16,128]{2,1,0:T(8,128)S(1)}, /*index=5*/s32[40,16...) while((s32[]{:T(128)}, f32[2,144,128]{2,0,1:T(2,128)S(1)}, ...), condition=%wide.region_9.12_spmd, body=%wide.region_0.11_spmd.sunk | while | flops 5675014 | bytes 7261843 | solution.py:135
  100.9 6.5 %collective-permute-start.12 = (f32[2,1,6,4,128]{4,2,3,1,0:T(8,128)S(1)}, f32[2,1,6,4,128]{4,2,3,1,0:T(8,128)S(1)}, u32[]{:S(2)}, u32[]{:S(2)}) collective-permute-start(f32[2,1,6,4,128]{4,2,3,1,0:T(8,128)S(1)} %slice.605), channel_id=1, source_target_pairs={{64,0},{128,64},{192,128},{256,192},{320,256},{384,320},{448,384},... | collective-permute-start | bytes 73736 | tf_op jit(solution)/shard_map/ppermute | solution.py:19
  107.5 9.3 %collective-permute-done.12 = f32[2,1,6,4,128]{4,2,3,1,0:T(8,128)S(1)} collective-permute-done((f32[2,1,6,4,128]{4,2,3,1,0:T(8,128)S(1)}, f32[2,1,6,4,128]{4,2,3,1,0:T(8,128)S(1)}, u32[]{:S(2)}, u32[]{:S(2)}) %collective-permute-start.12) | collective-permute-done | bytes 24608 | tf_op jit(solution)/shard_map/ppermute | solution.py:19
  116.7 6.2 %collective-permute-start.13 = (f32[2,1,6,4,128]{4,2,3,1,0:T(8,128)S(1)}, f32[2,1,6,4,128]{4,2,3,1,0:T(8,128)S(1)}, u32[]{:S(2)}, u32[]{:S(2)}) collective-permute-start(f32[2,1,6,4,128]{4,2,3,1,0:T(8,128)S(1)} %slice.607), channel_id=1, source_target_pairs={{0,64},{64,128},{128,192},{192,256},{256,320},{320,384},{384,448},... | collective-permute-start | bytes 73736 | tf_op jit(solution)/shard_map/ppermute | solution.py:19
  123.0 8.4 %collective-permute-done.13 = f32[2,1,6,4,128]{4,2,3,1,0:T(8,128)S(1)} collective-permute-done((f32[2,1,6,4,128]{4,2,3,1,0:T(8,128)S(1)}, f32[2,1,6,4,128]{4,2,3,1,0:T(8,128)S(1)}, u32[]{:S(2)}, u32[]{:S(2)}) %collective-permute-start.13) | collective-permute-done | bytes 24608 | tf_op jit(solution)/shard_map/ppermute | solution.py:19
  152.6 8.0 %collective-permute-start.18 = (f32[2,1,4,2,128]{4,2,3,1,0:T(4,128)S(1)}, f32[2,1,4,2,128]{4,2,3,1,0:T(4,128)S(1)}, u32[]{:S(2)}, u32[]{:S(2)}) collective-permute-start(f32[2,1,4,2,128]{4,2,3,1,0:T(4,128)S(1)} %get-tuple-element.906), channel_id=1, source_target_pairs={{0,64},{64,128},{128,192},{192,256},{256,320},{320,384},{384,448},... | collective-permute-start | bytes 24584 | tf_op jit(solution)/shard_map/ppermute | solution.py:29
  160.6 6.5 %collective-permute-start.19 = (f32[2,1,4,2,128]{4,2,3,1,0:T(4,128)S(1)}, f32[2,1,4,2,128]{4,2,3,1,0:T(4,128)S(1)}, u32[]{:S(2)}, u32[]{:S(2)}) collective-permute-start(f32[2,1,4,2,128]{4,2,3,1,0:T(4,128)S(1)} %get-tuple-element.907), channel_id=1, source_target_pairs={{64,0},{128,64},{192,128},{256,192},{320,256},{384,320},{448,384},... | collective-permute-start | bytes 24584 | tf_op jit(solution)/shard_map/ppermute | solution.py:30
  167.2 8.6 %collective-permute-done.19 = f32[2,1,4,2,128]{4,2,3,1,0:T(4,128)S(1)} collective-permute-done((f32[2,1,4,2,128]{4,2,3,1,0:T(4,128)S(1)}, f32[2,1,4,2,128]{4,2,3,1,0:T(4,128)S(1)}, u32[]{:S(2)}, u32[]{:S(2)}) %collective-permute-start.19) | collective-permute-done | bytes 8224 | tf_op jit(solution)/shard_map/ppermute | solution.py:30
  191.9 52.7 %while.49 = (s32[]{:T(128)}, f32[3,144,128]{2,0,1:T(4,128)S(1)}, s32[]{:T(128)}, s32[40]{0:T(128)S(1)}, s32[40,16,128]{2,1,0:T(8,128)S(1)}, /*index=5*/s32[40,16...) while((s32[]{:T(128)}, f32[3,144,128]{2,0,1:T(4,128)S(1)}, ...), condition=%wide.region_17.21_spmd, body=%wide.region_10.20_spmd.sunk | while | flops 8691590 | bytes 10348267 | solution.py:135
  244.6 5.6 collective-permute-start.24
  250.3 10.2 %collective-permute-done.24 = f32[3,1,6,4,128]{4,3,2,1,0:T(4,128)S(1)} collective-permute-done((f32[3,1,6,4,128]{4,3,2,1,0:T(4,128)S(1)}, f32[3,1,6,4,128]{4,3,2,1,0:T(4,128)S(1)}, u32[]{:S(2)}, u32[]{:S(2)}) %collective-permute-start.24) | collective-permute-done | bytes 36896 | tf_op jit(solution)/shard_map/ppermute | solution.py:19
  265.1 10.0 %collective-permute-done.25 = f32[3,1,6,4,128]{4,3,2,1,0:T(4,128)S(1)} collective-permute-done((f32[3,1,6,4,128]{4,3,2,1,0:T(4,128)S(1)}, f32[3,1,6,4,128]{4,3,2,1,0:T(4,128)S(1)}, u32[]{:S(2)}, u32[]{:S(2)}) %collective-permute-start.25) | collective-permute-done | bytes 36896 | tf_op jit(solution)/shard_map/ppermute | solution.py:19
  275.1 5.5 collective-permute-start.26
  298.5 5.3 collective-permute-start.30
  303.8 9.2 %collective-permute-start.31 = (f32[3,1,4,2,128]{4,3,2,1,0:T(2,128)S(1)}, f32[3,1,4,2,128]{4,3,2,1,0:T(2,128)S(1)}, u32[]{:S(2)}, u32[]{:S(2)}) collective-permute-start(f32[3,1,4,2,128]{4,3,2,1,0:T(2,128)S(1)} %get-tuple-element.899), channel_id=1, source_target_pairs={{64,0},{128,64},{192,128},{256,192},{320,256},{384,320},{448,384},... | collective-permute-start | bytes 36872 | tf_op jit(solution)/shard_map/ppermute | solution.py:30
  313.1 6.1 %collective-permute-done.31 = f32[3,1,4,2,128]{4,3,2,1,0:T(2,128)S(1)} collective-permute-done((f32[3,1,4,2,128]{4,3,2,1,0:T(2,128)S(1)}, f32[3,1,4,2,128]{4,3,2,1,0:T(2,128)S(1)}, u32[]{:S(2)}, u32[]{:S(2)}) %collective-permute-start.31) | collective-permute-done | bytes 12320 | tf_op jit(solution)/shard_map/ppermute | solution.py:30
  335.6 39.8 %while.50 = (s32[]{:T(128)}, f32[2,144,128]{2,0,1:T(2,128)S(1)}, s32[]{:T(128)}, s32[40]{0:T(128)S(1)}, s32[40,16,128]{2,1,0:T(8,128)S(1)}, /*index=5*/s32[40,16...) while((s32[]{:T(128)}, f32[2,144,128]{2,0,1:T(2,128)S(1)}, ...), condition=%wide.region_27.31_spmd, body=%wide.region_18.30_spmd.sunk | while | flops 5675014 | bytes 7261843 | solution.py:135
  375.4 8.2 %collective-permute-start.36 = (f32[2,1,6,4,128]{4,2,3,1,0:T(8,128)S(1)}, f32[2,1,6,4,128]{4,2,3,1,0:T(8,128)S(1)}, u32[]{:S(2)}, u32[]{:S(2)}) collective-permute-start(f32[2,1,6,4,128]{4,2,3,1,0:T(8,128)S(1)} %slice.642), channel_id=1, source_target_pairs={{64,0},{128,64},{192,128},{256,192},{320,256},{384,320},{448,384},... | collective-permute-start | bytes 73736 | tf_op jit(solution)/shard_map/ppermute | solution.py:19
  383.7 7.2 %collective-permute-done.36 = f32[2,1,6,4,128]{4,2,3,1,0:T(8,128)S(1)} collective-permute-done((f32[2,1,6,4,128]{4,2,3,1,0:T(8,128)S(1)}, f32[2,1,6,4,128]{4,2,3,1,0:T(8,128)S(1)}, u32[]{:S(2)}, u32[]{:S(2)}) %collective-permute-start.36) | collective-permute-done | bytes 24608 | tf_op jit(solution)/shard_map/ppermute | solution.py:19
  390.9 5.7 collective-permute-start.37
  396.6 8.8 %collective-permute-done.37 = f32[2,1,6,4,128]{4,2,3,1,0:T(8,128)S(1)} collective-permute-done((f32[2,1,6,4,128]{4,2,3,1,0:T(8,128)S(1)}, f32[2,1,6,4,128]{4,2,3,1,0:T(8,128)S(1)}, u32[]{:S(2)}, u32[]{:S(2)}) %collective-permute-start.37) | collective-permute-done | bytes 24608 | tf_op jit(solution)/shard_map/ppermute | solution.py:19
  405.4 5.9 %collective-permute-start.38 = (f32[2,4,1,4,128]{4,2,3,1,0:T(1,128)S(1)}, f32[2,4,1,4,128]{4,2,3,1,0:T(1,128)S(1)}, u32[]{:S(2)}, u32[]{:S(2)}) collective-permute-start(f32[2,4,1,4,128]{4,2,3,1,0:T(1,128)S(1)} %slice.647), channel_id=1, source_target_pairs={{8,0},{16,8},{24,16},{32,24},{40,32},{48,40},{56,48},{9,1},{17,9},... | collective-permute-start | bytes 49160 | tf_op jit(solution)/shard_map/ppermute | solution.py:19
  428.6 6.2 %collective-permute-start.42 = (f32[2,1,4,2,128]{4,2,3,1,0:T(4,128)S(1)}, f32[2,1,4,2,128]{4,2,3,1,0:T(4,128)S(1)}, u32[]{:S(2)}, u32[]{:S(2)}) collective-permute-start(f32[2,1,4,2,128]{4,2,3,1,0:T(4,128)S(1)} %get-tuple-element.904), channel_id=1, source_target_pairs={{0,64},{64,128},{128,192},{192,256},{256,320},{320,384},{384,448},... | collective-permute-start | bytes 24584 | tf_op jit(solution)/shard_map/ppermute | solution.py:29
  434.9 8.3 %collective-permute-start.43 = (f32[2,1,4,2,128]{4,2,3,1,0:T(4,128)S(1)}, f32[2,1,4,2,128]{4,2,3,1,0:T(4,128)S(1)}, u32[]{:S(2)}, u32[]{:S(2)}) collective-permute-start(f32[2,1,4,2,128]{4,2,3,1,0:T(4,128)S(1)} %get-tuple-element.905), channel_id=1, source_target_pairs={{64,0},{128,64},{192,128},{256,192},{320,256},{384,320},{448,384},... | collective-permute-start | bytes 24584 | tf_op jit(solution)/shard_map/ppermute | solution.py:30
  443.2 6.8 %collective-permute-done.43 = f32[2,1,4,2,128]{4,2,3,1,0:T(4,128)S(1)} collective-permute-done((f32[2,1,4,2,128]{4,2,3,1,0:T(4,128)S(1)}, f32[2,1,4,2,128]{4,2,3,1,0:T(4,128)S(1)}, u32[]{:S(2)}, u32[]{:S(2)}) %collective-permute-start.43) | collective-permute-done | bytes 8224 | tf_op jit(solution)/shard_map/ppermute | solution.py:30
  466.1 64.0 %while.51 = (s32[]{:T(128)}, f32[3,144,128]{2,0,1:T(4,128)S(1)}, s32[]{:T(128)}, s32[40]{0:T(128)S(1)}, s32[40,16,128]{2,1,0:T(8,128)S(1)}, /*index=5*/s32[40,16...) while((s32[]{:T(128)}, f32[3,144,128]{2,0,1:T(4,128)S(1)}, ...), condition=%wide.region_35.39_spmd, body=%wide.region_28.38_spmd.sunk | while | flops 8691590 | bytes 10351087 | solution.py:135
  530.1 7.4 %collective-permute-start.48 = (f32[3,1,6,4,128]{4,3,2,1,0:T(4,128)S(1)}, f32[3,1,6,4,128]{4,3,2,1,0:T(4,128)S(1)}, u32[]{:S(2)}, u32[]{:S(2)}) collective-permute-start(f32[3,1,6,4,128]{4,3,2,1,0:T(4,128)S(1)} %slice.660), channel_id=1, source_target_pairs={{64,0},{128,64},{192,128},{256,192},{320,256},{384,320},{448,384},... | collective-permute-start | bytes 110600 | tf_op jit(solution)/shard_map/ppermute | solution.py:19
  537.5 8.4 %collective-permute-done.48 = f32[3,1,6,4,128]{4,3,2,1,0:T(4,128)S(1)} collective-permute-done((f32[3,1,6,4,128]{4,3,2,1,0:T(4,128)S(1)}, f32[3,1,6,4,128]{4,3,2,1,0:T(4,128)S(1)}, u32[]{:S(2)}, u32[]{:S(2)}) %collective-permute-start.48) | collective-permute-done | bytes 36896 | tf_op jit(solution)/shard_map/ppermute | solution.py:19
  548.5 12.0 %collective-permute-done.49 = f32[3,1,6,4,128]{4,3,2,1,0:T(4,128)S(1)} collective-permute-done((f32[3,1,6,4,128]{4,3,2,1,0:T(4,128)S(1)}, f32[3,1,6,4,128]{4,3,2,1,0:T(4,128)S(1)}, u32[]{:S(2)}, u32[]{:S(2)}) %collective-permute-start.49) | collective-permute-done | bytes 36896 | tf_op jit(solution)/shard_map/ppermute | solution.py:19
  (1007 shorter events, 362.1 us)
Async XLA Ops:
  1.6 30.6 %collective-permute-start.6 = (f32[3,1,4,2,128]{4,3,2,1,0:T(2,128)S(1)}, f32[3,1,4,2,128]{4,3,2,1,0:T(2,128)S(1)}, u32[]{:S(2)}, u32[]{:S(2)}) collective-permute-start(f32[3,1,4,2,128]{4,3,2,1,0:T(2,128)S(1)} %get-tuple-element.902), channel_id=1, source_target_pairs={{0,64},{64,128},{128,192},{192,256},{256,320},{320,384},{384,448},... | collective-permute-start | bytes 36872 | tf_op jit(solution)/shard_map/ppermute | solution.py:29
  6.2 26.0 %collective-permute-start.7 = (f32[3,1,4,2,128]{4,3,2,1,0:T(2,128)S(1)}, f32[3,1,4,2,128]{4,3,2,1,0:T(2,128)S(1)}, u32[]{:S(2)}, u32[]{:S(2)}) collective-permute-start(f32[3,1,4,2,128]{4,3,2,1,0:T(2,128)S(1)} %get-tuple-element.903), channel_id=1, source_target_pairs={{64,0},{128,64},{192,128},{256,192},{320,256},{384,320},{448,384},... | collective-permute-start | bytes 36872 | tf_op jit(solution)/shard_map/ppermute | solution.py:30
  16.9 22.4 %collective-permute-start = (f32[4,1,4,2,128]{4,3,2,1,0:T(2,128)S(1)}, f32[4,1,4,2,128]{4,3,2,1,0:T(2,128)S(1)}, u32[]{:S(2)}, u32[]{:S(2)}) collective-permute-start(f32[4,1,4,2,128]{4,3,2,1,0:T(2,128)S(1)} %get-tuple-element.894), channel_id=1, source_target_pairs={{0,64},{64,128},{128,192},{192,256},{256,320},{320,384},{384,448},... | collective-permute-start | bytes 49160 | tf_op jit(solution)/shard_map/ppermute | solution.py:29
  22.4 16.9 %collective-permute-start.1 = (f32[4,1,4,2,128]{4,3,2,1,0:T(2,128)S(1)}, f32[4,1,4,2,128]{4,3,2,1,0:T(2,128)S(1)}, u32[]{:S(2)}, u32[]{:S(2)}) collective-permute-start(f32[4,1,4,2,128]{4,3,2,1,0:T(2,128)S(1)} %get-tuple-element.895), channel_id=1, source_target_pairs={{64,0},{128,64},{192,128},{256,192},{320,256},{384,320},{448,384},... | collective-permute-start | bytes 49160 | tf_op jit(solution)/shard_map/ppermute | solution.py:30
  32.2 14.9 %collective-permute-start.8 = (f32[3,6,1,2,128]{4,3,2,1,0:T(2,128)S(1)}, f32[3,6,1,2,128]{4,3,2,1,0:T(2,128)S(1)}, u32[]{:S(2)}, u32[]{:S(2)}) collective-permute-start(f32[3,6,1,2,128]{4,3,2,1,0:T(2,128)S(1)} %get-tuple-element.888), channel_id=1, source_target_pairs={{0,8},{8,16},{16,24},{24,32},{32,40},{40,48},{48,56},{1,9},{9,17},... | collective-permute-start | bytes 55304 | tf_op jit(solution)/shard_map/ppermute | solution.py:29
  35.2 12.0 %collective-permute-start.9 = (f32[3,6,1,2,128]{4,3,2,1,0:T(2,128)S(1)}, f32[3,6,1,2,128]{4,3,2,1,0:T(2,128)S(1)}, u32[]{:S(2)}, u32[]{:S(2)}) collective-permute-start(f32[3,6,1,2,128]{4,3,2,1,0:T(2,128)S(1)} %get-tuple-element.889), channel_id=1, source_target_pairs={{8,0},{16,8},{24,16},{32,24},{40,32},{48,40},{56,48},{9,1},{17,9},... | collective-permute-start | bytes 55304 | tf_op jit(solution)/shard_map/ppermute | solution.py:30
  40.1 12.8 %collective-permute-start.2 = (f32[4,6,1,2,128]{4,3,2,1,0:T(2,128)S(1)}, f32[4,6,1,2,128]{4,3,2,1,0:T(2,128)S(1)}, u32[]{:S(2)}, u32[]{:S(2)}) collective-permute-start(f32[4,6,1,2,128]{4,3,2,1,0:T(2,128)S(1)} %get-tuple-element.884), channel_id=1, source_target_pairs={{0,8},{8,16},{16,24},{24,32},{32,40},{40,48},{48,56},{1,9},{9,17},... | collective-permute-start | bytes 73736 | tf_op jit(solution)/shard_map/ppermute | solution.py:29
  42.2 10.7 %collective-permute-start.3 = (f32[4,6,1,2,128]{4,3,2,1,0:T(2,128)S(1)}, f32[4,6,1,2,128]{4,3,2,1,0:T(2,128)S(1)}, u32[]{:S(2)}, u32[]{:S(2)}) collective-permute-start(f32[4,6,1,2,128]{4,3,2,1,0:T(2,128)S(1)} %get-tuple-element.885), channel_id=1, source_target_pairs={{8,0},{16,8},{24,16},{32,24},{40,32},{48,40},{56,48},{9,1},{17,9},... | collective-permute-start | bytes 73736 | tf_op jit(solution)/shard_map/ppermute | solution.py:30
  47.3 11.4 %collective-permute-start.10 = (f32[3,6,6,1,128]{4,3,2,1,0:T(1,128)S(1)}, f32[3,6,6,1,128]{4,3,2,1,0:T(1,128)S(1)}, u32[]{:S(2)}, u32[]{:S(2)}) collective-permute-start(f32[3,6,6,1,128]{4,3,2,1,0:T(1,128)S(1)} %get-tuple-element.878), channel_id=1, source_target_pairs={{0,1},{1,2},{2,3},{3,4},{4,5},{5,6},{6,7},{8,9},{9,10},{10,11},{11... | collective-permute-start | bytes 165896 | tf_op jit(solution)/shard_map/ppermute | solution.py:29
  49.2 9.5 %collective-permute-start.11 = (f32[3,6,6,1,128]{4,3,2,1,0:T(1,128)S(1)}, f32[3,6,6,1,128]{4,3,2,1,0:T(1,128)S(1)}, u32[]{:S(2)}, u32[]{:S(2)}) collective-permute-start(f32[3,6,6,1,128]{4,3,2,1,0:T(1,128)S(1)} %get-tuple-element.879), channel_id=1, source_target_pairs={{1,0},{2,1},{3,2},{4,3},{5,4},{6,5},{7,6},{9,8},{10,9},{11,10},{12... | collective-permute-start | bytes 165896 | tf_op jit(solution)/shard_map/ppermute | solution.py:30
  100.9 15.8 %collective-permute-start.12 = (f32[2,1,6,4,128]{4,2,3,1,0:T(8,128)S(1)}, f32[2,1,6,4,128]{4,2,3,1,0:T(8,128)S(1)}, u32[]{:S(2)}, u32[]{:S(2)}) collective-permute-start(f32[2,1,6,4,128]{4,2,3,1,0:T(8,128)S(1)} %slice.605), channel_id=1, source_target_pairs={{64,0},{128,64},{192,128},{256,192},{320,256},{384,320},{448,384},... | collective-permute-start | bytes 73736 | tf_op jit(solution)/shard_map/ppermute | solution.py:19
  116.7 14.6 %collective-permute-start.13 = (f32[2,1,6,4,128]{4,2,3,1,0:T(8,128)S(1)}, f32[2,1,6,4,128]{4,2,3,1,0:T(8,128)S(1)}, u32[]{:S(2)}, u32[]{:S(2)}) collective-permute-start(f32[2,1,6,4,128]{4,2,3,1,0:T(8,128)S(1)} %slice.607), channel_id=1, source_target_pairs={{0,64},{64,128},{128,192},{192,256},{256,320},{320,384},{384,448},... | collective-permute-start | bytes 73736 | tf_op jit(solution)/shard_map/ppermute | solution.py:19
  152.6 14.6 %collective-permute-start.18 = (f32[2,1,4,2,128]{4,2,3,1,0:T(4,128)S(1)}, f32[2,1,4,2,128]{4,2,3,1,0:T(4,128)S(1)}, u32[]{:S(2)}, u32[]{:S(2)}) collective-permute-start(f32[2,1,4,2,128]{4,2,3,1,0:T(4,128)S(1)} %get-tuple-element.906), channel_id=1, source_target_pairs={{0,64},{64,128},{128,192},{192,256},{256,320},{320,384},{384,448},... | collective-permute-start | bytes 24584 | tf_op jit(solution)/shard_map/ppermute | solution.py:29
  160.6 15.2 %collective-permute-start.19 = (f32[2,1,4,2,128]{4,2,3,1,0:T(4,128)S(1)}, f32[2,1,4,2,128]{4,2,3,1,0:T(4,128)S(1)}, u32[]{:S(2)}, u32[]{:S(2)}) collective-permute-start(f32[2,1,4,2,128]{4,2,3,1,0:T(4,128)S(1)} %get-tuple-element.907), channel_id=1, source_target_pairs={{64,0},{128,64},{192,128},{256,192},{320,256},{384,320},{448,384},... | collective-permute-start | bytes 24584 | tf_op jit(solution)/shard_map/ppermute | solution.py:30
  175.8 7.1 %collective-permute-start.20 = (f32[2,6,1,2,128]{4,2,3,1,0:T(1,128)S(1)}, f32[2,6,1,2,128]{4,2,3,1,0:T(1,128)S(1)}, u32[]{:S(2)}, u32[]{:S(2)}) collective-permute-start(f32[2,6,1,2,128]{4,2,3,1,0:T(1,128)S(1)} %get-tuple-element.900), channel_id=1, source_target_pairs={{0,8},{8,16},{16,24},{24,32},{32,40},{40,48},{48,56},{1,9},{9,17},... | collective-permute-start | bytes 36872 | tf_op jit(solution)/shard_map/ppermute | solution.py:29
  244.6 15.9 %collective-permute-start.24 = (f32[3,1,6,4,128]{4,3,2,1,0:T(4,128)S(1)}, f32[3,1,6,4,128]{4,3,2,1,0:T(4,128)S(1)}, u32[]{:S(2)}, u32[]{:S(2)}) collective-permute-start(f32[3,1,6,4,128]{4,3,2,1,0:T(4,128)S(1)} %slice.623), channel_id=1, source_target_pairs={{64,0},{128,64},{192,128},{256,192},{320,256},{384,320},{448,384},... | collective-permute-start | bytes 110600 | tf_op jit(solution)/shard_map/ppermute | solution.py:19
  260.5 14.6 %collective-permute-start.25 = (f32[3,1,6,4,128]{4,3,2,1,0:T(4,128)S(1)}, f32[3,1,6,4,128]{4,3,2,1,0:T(4,128)S(1)}, u32[]{:S(2)}, u32[]{:S(2)}) collective-permute-start(f32[3,1,6,4,128]{4,3,2,1,0:T(4,128)S(1)} %slice.625), channel_id=1, source_target_pairs={{0,64},{64,128},{128,192},{192,256},{256,320},{320,384},{384,448},... | collective-permute-start | bytes 110600 | tf_op jit(solution)/shard_map/ppermute | solution.py:19
  275.1 7.0 %collective-permute-start.26 = (f32[3,4,1,4,128]{4,3,2,1,0:T(4,128)S(1)}, f32[3,4,1,4,128]{4,3,2,1,0:T(4,128)S(1)}, u32[]{:S(2)}, u32[]{:S(2)}) collective-permute-start(f32[3,4,1,4,128]{4,3,2,1,0:T(4,128)S(1)} %slice.628), channel_id=1, source_target_pairs={{8,0},{16,8},{24,16},{32,24},{40,32},{48,40},{56,48},{9,1},{17,9},... | collective-permute-start | bytes 73736 | tf_op jit(solution)/shard_map/ppermute | solution.py:19
  282.1 7.2 %collective-permute-start.27 = (f32[3,4,1,4,128]{4,3,2,1,0:T(4,128)S(1)}, f32[3,4,1,4,128]{4,3,2,1,0:T(4,128)S(1)}, u32[]{:S(2)}, u32[]{:S(2)}) collective-permute-start(f32[3,4,1,4,128]{4,3,2,1,0:T(4,128)S(1)} %slice.630), channel_id=1, source_target_pairs={{0,8},{8,16},{16,24},{24,32},{32,40},{40,48},{48,56},{1,9},{9,17},... | collective-permute-start | bytes 73736 | tf_op jit(solution)/shard_map/ppermute | solution.py:19
  298.5 14.6 %collective-permute-start.30 = (f32[3,1,4,2,128]{4,3,2,1,0:T(2,128)S(1)}, f32[3,1,4,2,128]{4,3,2,1,0:T(2,128)S(1)}, u32[]{:S(2)}, u32[]{:S(2)}) collective-permute-start(f32[3,1,4,2,128]{4,3,2,1,0:T(2,128)S(1)} %get-tuple-element.898), channel_id=1, source_target_pairs={{0,64},{64,128},{128,192},{192,256},{256,320},{320,384},{384,448},... | collective-permute-start | bytes 36872 | tf_op jit(solution)/shard_map/ppermute | solution.py:29
  303.8 15.3 %collective-permute-start.31 = (f32[3,1,4,2,128]{4,3,2,1,0:T(2,128)S(1)}, f32[3,1,4,2,128]{4,3,2,1,0:T(2,128)S(1)}, u32[]{:S(2)}, u32[]{:S(2)}) collective-permute-start(f32[3,1,4,2,128]{4,3,2,1,0:T(2,128)S(1)} %get-tuple-element.899), channel_id=1, source_target_pairs={{64,0},{128,64},{192,128},{256,192},{320,256},{384,320},{448,384},... | collective-permute-start | bytes 36872 | tf_op jit(solution)/shard_map/ppermute | solution.py:30
  319.2 7.1 %collective-permute-start.32 = (f32[3,6,1,2,128]{4,3,2,1,0:T(2,128)S(1)}, f32[3,6,1,2,128]{4,3,2,1,0:T(2,128)S(1)}, u32[]{:S(2)}, u32[]{:S(2)}) collective-permute-start(f32[3,6,1,2,128]{4,3,2,1,0:T(2,128)S(1)} %get-tuple-element.886), channel_id=1, source_target_pairs={{0,8},{8,16},{16,24},{24,32},{32,40},{40,48},{48,56},{1,9},{9,17},... | collective-permute-start | bytes 55304 | tf_op jit(solution)/shard_map/ppermute | solution.py:29
  375.4 15.4 %collective-permute-start.36 = (f32[2,1,6,4,128]{4,2,3,1,0:T(8,128)S(1)}, f32[2,1,6,4,128]{4,2,3,1,0:T(8,128)S(1)}, u32[]{:S(2)}, u32[]{:S(2)}) collective-permute-start(f32[2,1,6,4,128]{4,2,3,1,0:T(8,128)S(1)} %slice.642), channel_id=1, source_target_pairs={{64,0},{128,64},{192,128},{256,192},{320,256},{384,320},{448,384},... | collective-permute-start | bytes 73736 | tf_op jit(solution)/shard_map/ppermute | solution.py:19
  390.9 14.5 %collective-permute-start.37 = (f32[2,1,6,4,128]{4,2,3,1,0:T(8,128)S(1)}, f32[2,1,6,4,128]{4,2,3,1,0:T(8,128)S(1)}, u32[]{:S(2)}, u32[]{:S(2)}) collective-permute-start(f32[2,1,6,4,128]{4,2,3,1,0:T(8,128)S(1)} %slice.644), channel_id=1, source_target_pairs={{0,64},{64,128},{128,192},{192,256},{256,320},{320,384},{384,448},... | collective-permute-start | bytes 73736 | tf_op jit(solution)/shard_map/ppermute | solution.py:19
  405.4 7.3 %collective-permute-start.38 = (f32[2,4,1,4,128]{4,2,3,1,0:T(1,128)S(1)}, f32[2,4,1,4,128]{4,2,3,1,0:T(1,128)S(1)}, u32[]{:S(2)}, u32[]{:S(2)}) collective-permute-start(f32[2,4,1,4,128]{4,2,3,1,0:T(1,128)S(1)} %slice.647), channel_id=1, source_target_pairs={{8,0},{16,8},{24,16},{32,24},{40,32},{48,40},{56,48},{9,1},{17,9},... | collective-permute-start | bytes 49160 | tf_op jit(solution)/shard_map/ppermute | solution.py:19
  412.8 7.1 %collective-permute-start.39 = (f32[2,4,1,4,128]{4,2,3,1,0:T(1,128)S(1)}, f32[2,4,1,4,128]{4,2,3,1,0:T(1,128)S(1)}, u32[]{:S(2)}, u32[]{:S(2)}) collective-permute-start(f32[2,4,1,4,128]{4,2,3,1,0:T(1,128)S(1)} %slice.649), channel_id=1, source_target_pairs={{0,8},{8,16},{16,24},{24,32},{32,40},{40,48},{48,56},{1,9},{9,17},... | collective-permute-start | bytes 49160 | tf_op jit(solution)/shard_map/ppermute | solution.py:19
  428.6 14.6 %collective-permute-start.42 = (f32[2,1,4,2,128]{4,2,3,1,0:T(4,128)S(1)}, f32[2,1,4,2,128]{4,2,3,1,0:T(4,128)S(1)}, u32[]{:S(2)}, u32[]{:S(2)}) collective-permute-start(f32[2,1,4,2,128]{4,2,3,1,0:T(4,128)S(1)} %get-tuple-element.904), channel_id=1, source_target_pairs={{0,64},{64,128},{128,192},{192,256},{256,320},{320,384},{384,448},... | collective-permute-start | bytes 24584 | tf_op jit(solution)/shard_map/ppermute | solution.py:29
  434.9 15.2 %collective-permute-start.43 = (f32[2,1,4,2,128]{4,2,3,1,0:T(4,128)S(1)}, f32[2,1,4,2,128]{4,2,3,1,0:T(4,128)S(1)}, u32[]{:S(2)}, u32[]{:S(2)}) collective-permute-start(f32[2,1,4,2,128]{4,2,3,1,0:T(4,128)S(1)} %get-tuple-element.905), channel_id=1, source_target_pairs={{64,0},{128,64},{192,128},{256,192},{320,256},{384,320},{448,384},... | collective-permute-start | bytes 24584 | tf_op jit(solution)/shard_map/ppermute | solution.py:30
  450.0 7.1 %collective-permute-start.44 = (f32[2,6,1,2,128]{4,2,3,1,0:T(1,128)S(1)}, f32[2,6,1,2,128]{4,2,3,1,0:T(1,128)S(1)}, u32[]{:S(2)}, u32[]{:S(2)}) collective-permute-start(f32[2,6,1,2,128]{4,2,3,1,0:T(1,128)S(1)} %get-tuple-element.896), channel_id=1, source_target_pairs={{0,8},{8,16},{16,24},{24,32},{32,40},{40,48},{48,56},{1,9},{9,17},... | collective-permute-start | bytes 36872 | tf_op jit(solution)/shard_map/ppermute | solution.py:29
  530.1 15.8 %collective-permute-start.48 = (f32[3,1,6,4,128]{4,3,2,1,0:T(4,128)S(1)}, f32[3,1,6,4,128]{4,3,2,1,0:T(4,128)S(1)}, u32[]{:S(2)}, u32[]{:S(2)}) collective-permute-start(f32[3,1,6,4,128]{4,3,2,1,0:T(4,128)S(1)} %slice.660), channel_id=1, source_target_pairs={{64,0},{128,64},{192,128},{256,192},{320,256},{384,320},{448,384},... | collective-permute-start | bytes 110600 | tf_op jit(solution)/shard_map/ppermute | solution.py:19
  546.0 14.6 %collective-permute-start.49 = (f32[3,1,6,4,128]{4,3,2,1,0:T(4,128)S(1)}, f32[3,1,6,4,128]{4,3,2,1,0:T(4,128)S(1)}, u32[]{:S(2)}, u32[]{:S(2)}) collective-permute-start(f32[3,1,6,4,128]{4,3,2,1,0:T(4,128)S(1)} %slice.662), channel_id=1, source_target_pairs={{0,64},{64,128},{128,192},{192,256},{256,320},{320,384},{384,448},... | collective-permute-start | bytes 110600 | tf_op jit(solution)/shard_map/ppermute | solution.py:19
  567.2 7.2 %collective-permute-start.51 = (f32[3,4,1,4,128]{4,3,2,1,0:T(4,128)S(1)}, f32[3,4,1,4,128]{4,3,2,1,0:T(4,128)S(1)}, u32[]{:S(2)}, u32[]{:S(2)}) collective-permute-start(f32[3,4,1,4,128]{4,3,2,1,0:T(4,128)S(1)} %slice.667), channel_id=1, source_target_pairs={{0,8},{8,16},{16,24},{24,32},{32,40},{40,48},{48,56},{1,9},{9,17},... | collective-permute-start | bytes 73736 | tf_op jit(solution)/shard_map/ppermute | solution.py:19
  (66 other events, 344.8 us)
where the time goes:
time: 587 us; the launch traced here: 584 us
  starting transfers between devices  226 us (39%)
  waiting for transfers between devices  151 us (26%)
  other arithmetic  124 us (21%)
  local copies, waits for them, and re-layouts  75.2 us (13%)
    ppermute x24, waiting for transfers between devices, shifted(): lax.ppermute(value, axis, [(source, source + steps) for source in range(l...  119 us
    ppermute x24, starting transfers between devices, shifted(): lax.ppermute(value, axis, [(source, source + steps) for source in range(l...  90.5 us
    ppermute x15, starting transfers between devices, with_halo(): after = lax.ppermute(leading, axis, down)  86 us
    ppermute x15, starting transfers between devices, with_halo(): before = lax.ppermute(last, axis, up)  50.1 us
    ppermute x15, waiting for transfers between devices, with_halo(): after = lax.ppermute(leading, axis, down)  32.3 us
    reduce_sum x10, other arithmetic, force_terms(): far_terms = -jnp.sum(bond_force * near_volume[None, :, :, None], axis=2)  16 us
    scatter-add x20, other arithmetic, group_step(): running = running.at[:, own_block].add(near_terms)  15.7 us
    scatter-add x20, other arithmetic, group_step(): return running.at[:, partner_block].add(far_terms)  15.6 us
  transfers between devices with their start and end apart: 54, of which 34 were waited for; matrix products, arithmetic and copies ran while one was open for 0% of the time, Pallas kernels for 0%

commit v1 on v0

v1 whole, which is shorter than its diff:
```python
import functools

import jax
import jax.numpy as jnp
from jax import lax
from jax.experimental import pallas as pl
from jax.experimental.pallas import tpu as pltpu
from jax.sharding import PartitionSpec as P

BLK = 128
WORDS = 16
BX, BY, BZ = 4, 4, 2
TILES = 40
N_DEV = 8
K_BULK = 8000.0
MU_SHEAR = 600.0
VOLUME_FLOOR = 2000.0
TIME_DELTA = 0.05
TINY = 1e-30
UNROLL = 4
ROWS = (BY + 2) * (BZ + 2) * 8

YZ = [(-1, 0), (1, 0), (0, -1), (0, 1), (-1, -1), (-1, 1), (1, -1), (1, 1)]
OWN_ROWS = BY * BZ * 8
GHOST = dict(zip(YZ, (slice(64, 80), slice(80, 96), slice(96, 128), slice(128, 160), slice(160, 168), slice(168, 176), slice(176, 184), slice(184, 192))))
INNER = {
    (-1, 0): (0, 1),
    (1, 0): (6, 7),
    (0, -1): (0, 2, 4, 6),
    (0, 1): (1, 3, 5, 7),
    (-1, -1): (0,),
    (-1, 1): (1,),
    (1, -1): (6,),
    (1, 1): (7,),
}


def slot(step):
    rows = GHOST[step]
    return slice(rows.start - OWN_ROWS, rows.stop - OWN_ROWS)


def column(g):
    return slice(g * 8, g * 8 + 8)


def plane(x):
    return pl.ds(x, 8, stride=8)


def kernel(
    pos,
    vol,
    dis,
    vel,
    acc,
    own,
    par,
    cnt,
    fam_hbm,
    brk_hbm,
    out_u,
    out_v,
    out_a,
    fam,
    brk,
    near_at,
    far_at,
    data,
    xrel,
    ypos,
    half,
    base,
    inv,
    kap,
    w_ref,
    r_ref,
    e_ref,
    n_ref,
    col_x,
    col_y,
    col_c,
    hot_t,
    hot,
    terms,
    sum_s1,
    sum_f1,
    sum_s2,
    sum_f2,
    coef1,
    coef2,
    disp2,
    fold_s1,
    fold_f1,
    fold_s2,
    fold_f2,
    zs0,
    zs1,
    zs2,
    zs3,
    xs0,
    xr0,
    xsb,
    xrb,
    xs1,
    xr1,
    xs2,
    xr2,
    xs3,
    xr3,
    xs4,
    xr4,
    send_sem,
    recv_sem,
    load_sem,
):
    gx, gy, gz = lax.axis_index("gx"), lax.axis_index("gy"), lax.axis_index("gz")
    sent = []
    counter = [0]

    def there(step):
        ok = None
        for at, d in zip((gx, gy, gz), step):
            if d:
                test = at > 0 if d < 0 else at < N_DEV - 1
                ok = test if ok is None else jnp.logical_and(ok, test)
        return ok

    def target(step):
        return tuple(at + d for at, d in zip((gx, gy, gz), step))

    class Exchange:
        def __init__(self, steps, source, sink):
            self.steps, self.base = steps, counter[0]
            counter[0] += len(steps)
            self.source, self.sink = source, sink
            sent.append(self)

        def copy(self, i, step, back):
            opposite = tuple(-d for d in step)
            return pltpu.make_async_remote_copy(
                src_ref=self.source(step),
                dst_ref=self.sink(step if back else opposite),
                send_sem=send_sem.at[self.base + i],
                recv_sem=recv_sem.at[self.base + (i if back else self.steps.index(opposite))],
                device_id=target(step),
                device_id_type=pl.DeviceIdType.MESH,
            )

        def start(self):
            for i, step in enumerate(self.steps):
                pl.when(there(step))(lambda i=i, step=step: self.copy(i, step, False).start())

        def arrive(self):
            for i, step in enumerate(self.steps):
                pl.when(there(step))(lambda i=i, step=step: self.copy(i, step, True).wait_recv())

        def finish(self):
            for i, step in enumerate(self.steps):
                pl.when(there(step))(lambda i=i, step=step: self.copy(i, step, False).wait_send())

    yz_steps = [(0, dy, dz) for dy, dz in YZ]
    x_steps = [(-1, 0, 0), (1, 0, 0)]

    def fold_exchange(sums, fold):
        return Exchange(
            yz_steps,
            lambda s: sums.at[:, GHOST[s[1:]]],
            lambda s: fold.at[:, slot(s[1:])],
        )

    def add_folds(sums, fold, channels):
        for c in range(channels):
            for g in range(BY * BZ):
                total = sums[c, column(g)]
                for step in YZ:
                    if g in INNER[step]:
                        first = slot(step).start + INNER[step].index(g) * 8
                        total = total + fold[c, first : first + 8]
                sums[c, column(g)] = total

    def halo_exchange(array, packed, channels):
        def source(s):
            step = s[1:]
            if step[0] == 0:
                return packed.at[(step[1] + 1) // 2]
            groups = INNER[step]
            return array.at[:, groups[0] * 8 : groups[-1] * 8 + 8]

        for side in (0, 1):
            for j in range(BY):
                for c in range(channels):
                    packed[side, c, column(j)] = array[c, column(2 * j + side)]
        return Exchange(yz_steps, source, lambda s: array.at[:, GHOST[s[1:]]])

    def x_exchange(send, recv):
        return Exchange(
            x_steps, lambda s: send.at[(s[0] + 1) // 2], lambda s: recv.at[(s[0] + 1) // 2]
        )

    def shared(side):
        return ((0, 1), (BX, BX + 1))[side]

    def pack_x(send, array, channels):
        for side in (0, 1):
            for c in range(channels):
                for j, x in enumerate(shared(side)):
                    send[side, c, column(j)] = array[c, plane(x), :]

    def add_x(array, recv, channels):
        for side in (0, 1):
            for c in range(channels):
                for j, x in enumerate(shared(side)):
                    array[c, plane(x), :] = array[c, plane(x), :] + recv[side, c, column(j)]

    barrier = pltpu.get_barrier_semaphore()
    expected = jnp.int32(0)
    for step in x_steps + yz_steps:
        expected = expected + there(step).astype(jnp.int32)

        @pl.when(there(step))
        def _(step=step):
            pl.semaphore_signal(
                barrier, inc=1, device_id=target(step), device_id_type=pl.DeviceIdType.MESH
            )

    load_f = pltpu.make_async_copy(fam_hbm, fam, load_sem.at[0])
    load_b = pltpu.make_async_copy(brk_hbm, brk, load_sem.at[1])
    load_f.start()
    load_b.start()

    for x in range(BX):
        data[3, plane(x + 1), :] = vol[x]
        for k in range(3):
            data[k, plane(x + 1), :] = pos[k, x]
            h = vel[k, x] + 0.5 * TIME_DELTA * acc[k, x]
            u1 = dis[k, x] + TIME_DELTA * h
            data[4 + k, plane(x + 1), :] = u1
            half[k, x] = h
            base[k, plane(x + 1), :] = u1 + TIME_DELTA * h
    for side, x in ((0, 1), (1, BX)):
        for c in range(7):
            xs0[side, c] = data[c, plane(x), :]
        for c in range(3):
            xsb[side, c] = base[c, plane(x), :]

    pl.semaphore_wait(barrier, expected)
    x0 = x_exchange(xs0, xr0)
    xb = x_exchange(xsb, xrb)
    x0.start()

    for side, step in enumerate(x_steps):

        @pl.when(jnp.logical_not(there(step)))
        def _(side=side):
            for ref in (xr0, xrb, xr1, xr2, xr3, xr4):
                ref[side] = jnp.zeros(ref.shape[1:], jnp.float32)

    for step in YZ:

        @pl.when(jnp.logical_not(there((0,) + step)))
        def _(step=step):
            for ref in (data, coef1, disp2, coef2):
                rows = GHOST[step]
                ref[:, rows] = jnp.zeros((ref.shape[0], rows.stop - rows.start, BLK), jnp.float32)
            for ref in (fold_s1, fold_f1, fold_s2, fold_f2):
                rows = slot(step)
                ref[:, rows] = jnp.zeros((ref.shape[0], rows.stop - rows.start, BLK), jnp.float32)

    terms[...] = jnp.zeros_like(terms)
    hot_t[...] = jnp.zeros_like(hot_t)
    org = [g.astype(jnp.float32) * 16.0 for g in (gx, gy, gz)]
    load_f.wait()
    load_b.wait()
    sub = lax.broadcasted_iota(jnp.int32, (BLK, BLK), 0)
    lane = lax.broadcasted_iota(jnp.int32, (BLK, BLK), 1)

    def row_of(block):
        x, g = block // 24, block % 24
        y, z = g // 4, g % 4
        inside_y, inside_z = (y >= 1) & (y <= BY), (z >= 1) & (z <= BZ)
        upper_y, upper_z = (y > BY).astype(jnp.int32), (z > BZ).astype(jnp.int32)
        at_y = jnp.where(inside_z, 8 + 2 * upper_y + z - 1, 20 + 2 * upper_y + upper_z)
        in_y = jnp.where(inside_z, (y - 1) * 2 + z - 1, 12 + 4 * upper_z + y - 1)
        return jnp.where(inside_y, in_y, at_y) * 8 + x

    def mask_body(t, carry):
        a, b = own[t], par[t]
        row_a, row_b = row_of(a), row_of(b)
        near_at[t] = jnp.clip(row_a // 8 * BX + row_a % 8 - 1, 0, BX * BY * BZ - 1)
        far_at[t] = jnp.clip(row_b, 0, ROWS - 1)
        apart = (a != b).astype(jnp.int32)
        live = (t < cnt[0, 0, 0]).astype(jnp.int32)
        shift = lax.broadcasted_iota(jnp.int32, (8, BLK), 0)
        rows = []
        for g in range(WORDS):
            word = fam[t, pl.ds(g, 1), :] & ~brk[t, pl.ds(g, 1), :]
            rows.append((jnp.broadcast_to(word, (8, BLK)) >> shift) & 1)
        bits = jnp.concatenate(rows, axis=0)
        bits = bits & ((sub > lane).astype(jnp.int32) | apart) & live
        w_ref[t] = bits.astype(jnp.float32).T
        code = lax.broadcasted_iota(jnp.int32, (1, BLK), 1)
        for half_at in range(2):
            hot_t[half_at, pl.ds(2 * t, 1), :] = (code + 128 * half_at == row_a).astype(jnp.float32)
            hot_t[half_at, pl.ds(2 * t + 1, 1), :] = (code + 128 * half_at == row_b).astype(
                jnp.float32
            )
        return carry

    lax.fori_loop(0, TILES, mask_body, 0, unroll=UNROLL)
    picked = jnp.concatenate([hot_t[0].T, hot_t[1].T], axis=0)[0:ROWS].astype(jnp.bfloat16)
    hot[:, 0:128] = picked
    hot[:, 128:256] = picked

    def put_columns(dest, first, values):
        def body(g, carry):
            rows = pl.ds(pl.multiple_of(g * 8, 8), 8)
            for k, value in enumerate(values(rows)):
                turned = value.T
                for x in range(BX):
                    dest[g * BX + x, first + k] = jnp.broadcast_to(
                        turned[:, x + 1 : x + 2], (BLK, BLK)
                    )
            return carry

        lax.fori_loop(0, BY * BZ, body, 0)

    put_columns(
        col_x, 0, lambda rows: [data[k, rows, :] - org[k] for k in range(3)] + [data[3, rows, :]]
    )
    put_columns(
        col_y,
        0,
        lambda rows: [(data[k, rows, :] - org[k]) + data[4 + k, rows, :] for k in range(3)],
    )

    x0.arrive()
    for side, x in ((0, 0), (1, BX + 1)):
        for c in range(7):
            data[c, plane(x), :] = xr0[side, c]
    h0 = halo_exchange(data, zs0, 7)
    h0.start()
    xb.start()
    volume = data[3, 0:OWN_ROWS]
    inv[...] = jnp.where(volume > 0.0, 1.0 / jnp.where(volume > 0.0, volume, 1.0), 0.0)
    h0.arrive()
    for k in range(3):
        xrel[k] = data[k] - org[k]
        ypos[k] = xrel[k] + data[4 + k]

    def far_row(ref, k, at):
        return ref[k, pl.ds(at, 1), :]

    diagonal = sub == lane

    def put_sums(t, c, values, far_sign=1):
        per_a = jnp.sum(values, axis=1, keepdims=True)
        near = jnp.sum(jnp.where(diagonal, per_a, 0.0), axis=0, keepdims=True)
        far = jnp.sum(values, axis=0, keepdims=True)
        terms[c, pl.ds(2 * t, 1), :] = near
        terms[c, pl.ds(2 * t + 1, 1), :] = far if far_sign > 0 else -far

    def gather_sums(sums, channels):
        full = jnp.concatenate([terms[c] for c in range(channels)], axis=1)
        high = full.astype(jnp.bfloat16)
        low = (full - high.astype(jnp.float32)).astype(jnp.bfloat16)
        out = jnp.dot(
            hot[...], jnp.concatenate([high, low], axis=0), preferred_element_type=jnp.float32
        )
        for c in range(channels):
            sums[c] = out[:, c * 128 : (c + 1) * 128]

    def deformed(near, at):
        d = [far_row(ypos, k, at) - col_y[near, k] for k in range(3)]
        square = jnp.maximum(d[0] * d[0] + d[1] * d[1] + d[2] * d[2], TINY)
        inverse = lax.rsqrt(square)
        return d, square * inverse, inverse

    def first_body(t, carry):
        near, at = near_at[t], far_at[t]
        o = [far_row(xrel, k, at) - col_x[near, k] for k in range(3)]
        square = jnp.maximum(o[0] * o[0] + o[1] * o[1] + o[2] * o[2], TINY)
        rest = square * lax.rsqrt(square)
        weight = w_ref[t] * (col_x[near, 3] * far_row(data, 3, at))
        w_ref[t] = weight
        r_ref[t] = rest
        weighted = weight * rest
        put_sums(t, 1, weighted * rest)
        _, length, _ = deformed(near, at)
        put_sums(t, 0, weighted * (length - rest))
        return carry

    def sum_body(t, carry):
        near, at = near_at[t], far_at[t]
        _, length, _ = deformed(near, at)
        rest = r_ref[t]
        put_sums(t, 0, w_ref[t] * rest * (length - rest))
        return carry

    def geometry_body(t, carry):
        near, at = near_at[t], far_at[t]
        d, length, inverse = deformed(near, at)
        e_ref[t] = length - r_ref[t]
        scale = w_ref[t] * inverse
        for k in range(3):
            n_ref[t, k] = scale * d[k]
        return carry

    def force_body(far_p, t, carry):
        near, at = near_at[t], far_at[t]
        c = r_ref[t] * (col_c[near, 0] + far_row(far_p, 0, at))
        c = c + e_ref[t] * (col_c[near, 1] + far_row(coef1, 1, at))
        for k in range(3):
            put_sums(t, k, c * n_ref[t, k], far_sign=-1)
        return carry

    def tiles(body):
        lax.fori_loop(0, TILES, body, 0, unroll=UNROLL)

    own_rows = slice(0, OWN_ROWS)

    tiles(first_body)
    gather_sums(sum_s1, 2)
    f = fold_exchange(sum_s1, fold_s1)
    f.start()
    f.arrive()
    add_folds(sum_s1, fold_s1, 2)
    pack_x(xs1, sum_s1, 2)
    x1 = x_exchange(xs1, xr1)
    x1.start()
    tiles(geometry_body)
    x1.arrive()
    add_x(sum_s1, xr1, 2)
    floored = jnp.maximum(sum_s1[1, own_rows] * inv[...], VOLUME_FLOOR)
    kap[...] = (3.0 * (3.0 * K_BULK - 5.0 * MU_SHEAR)) * inv[...] / floored / floored
    coef1[0, own_rows] = sum_s1[0, own_rows] * kap[...]
    coef1[1, own_rows] = 15.0 * MU_SHEAR / floored
    h1 = halo_exchange(coef1, zs1, 2)
    h1.start()
    put_columns(col_c, 0, lambda rows: [coef1[k, rows, :] for k in range(2)])
    h1.arrive()

    tiles(functools.partial(force_body, coef1))
    gather_sums(sum_f1, 3)
    f = fold_exchange(sum_f1, fold_f1)
    f.start()
    xb.arrive()
    for side, x in ((0, 0), (1, BX + 1)):
        for k in range(3):
            base[k, plane(x), :] = xrb[side, k]
    f.arrive()
    add_folds(sum_f1, fold_f1, 3)
    pack_x(xs2, sum_f1, 3)
    x2 = x_exchange(xs2, xr2)
    x2.start()
    x2.arrive()
    add_x(sum_f1, xr2, 3)
    for k in range(3):
        force = sum_f1[k, own_rows] * inv[...]
        sum_f1[k, own_rows] = force
        disp2[k, own_rows] = base[k] + (TIME_DELTA * TIME_DELTA) * force
    h2 = halo_exchange(disp2, zs2, 3)
    h2.start()
    put_columns(
        col_y, 0, lambda rows: [xrel[k, rows, :] + disp2[k, rows, :] for k in range(3)]
    )
    for x in range(BX):
        for k in range(3):
            half[k, x] = half[k, x] + TIME_DELTA * sum_f1[k, plane(x + 1), :]
    h2.arrive()
    for k in range(3):
        ypos[k] = xrel[k] + disp2[k]

    tiles(sum_body)
    gather_sums(sum_s2, 1)
    f = fold_exchange(sum_s2, fold_s2)
    f.start()
    f.arrive()
    add_folds(sum_s2, fold_s2, 1)
    pack_x(xs3, sum_s2, 1)
    x3 = x_exchange(xs3, xr3)
    x3.start()
    tiles(geometry_body)
    x3.arrive()
    add_x(sum_s2, xr3, 1)
    coef2[0, own_rows] = sum_s2[0, own_rows] * kap[...]
    h3 = halo_exchange(coef2, zs3, 1)
    h3.start()
    put_columns(col_c, 0, lambda rows: [coef2[0, rows, :]])
    h3.arrive()

    tiles(functools.partial(force_body, coef2))
    gather_sums(sum_f2, 3)
    f = fold_exchange(sum_f2, fold_f2)
    f.start()
    f.arrive()
    add_folds(sum_f2, fold_f2, 3)
    for side, x in ((0, 0), (1, BX + 1)):
        for k in range(3):
            xs4[side, k] = sum_f2[k, plane(x), :]
    x4 = x_exchange(xs4, xr4)
    x4.start()
    for x in range(BX):
        for k in range(3):
            out_u[k, x] = disp2[k, plane(x + 1), :]
    x4.arrive()
    for x in range(BX):
        for k in range(3):
            force = sum_f2[k, plane(x + 1), :]
            if x == 0:
                force = force + xr4[0, k]
            if x == BX - 1:
                force = force + xr4[1, k]
            force = force * inv[plane(x + 1), :]
            out_a[k, x] = force
            out_v[k, x] = half[k, x] + 0.5 * TIME_DELTA * force
    for exchange in sent:
        exchange.finish()


def per_device(
    positions,
    volume,
    displacement,
    velocity,
    acceleration,
    tile_own,
    tile_partner,
    tile_count,
    family_bits,
    broken_bits,
):
    vmem = pl.BlockSpec(memory_space=pltpu.VMEM)
    smem = pl.BlockSpec(memory_space=pltpu.SMEM)
    hbm = pl.BlockSpec(memory_space=pl.ANY)
    out = jax.ShapeDtypeStruct((3, BX, BY * BZ, BLK), jnp.float32)

    def buf(*shape, dtype=jnp.float32):
        return pltpu.VMEM(shape, dtype)

    def grid(channels):
        return buf(channels, ROWS, BLK)

    def fold(channels):
        return buf(channels, ROWS - OWN_ROWS, BLK)

    def pair(channels, rows):
        return [buf(2, channels, rows, BLK), buf(2, channels, rows, BLK)]

    bits = pltpu.VMEM((TILES, WORDS, BLK), jnp.int32)
    copies = 8 * len(YZ) + 6 * 2
    values = (positions, displacement, velocity, acceleration)
    pos, dis, vel, acc = (v.reshape(3, BX, BY * BZ, BLK) for v in values)
    outs = pl.pallas_call(
        kernel,
        out_shape=[out] * 3,
        in_specs=[vmem] * 5 + [smem] * 3 + [hbm] * 2,
        out_specs=[vmem] * 3,
        scratch_shapes=[
            bits,
            bits,
            pltpu.SMEM((TILES,), jnp.int32),
            pltpu.SMEM((TILES,), jnp.int32),
            grid(7),
            grid(3),
            grid(3),
            buf(3, BX, BY * BZ, BLK),
            buf(3, OWN_ROWS, BLK),
            buf(OWN_ROWS, BLK),
            buf(OWN_ROWS, BLK),
            buf(TILES, BLK, BLK),
            buf(TILES, BLK, BLK),
            buf(TILES, BLK, BLK),
            buf(TILES, 3, BLK, BLK),
            buf(BX * BY * BZ, 4, BLK, BLK),
            buf(BX * BY * BZ, 3, BLK, BLK),
            buf(BX * BY * BZ, 2, BLK, BLK),
            buf(2, 128, 128),
            buf(ROWS, 256, dtype=jnp.bfloat16),
            buf(3, 128, 128),
            grid(2),
            grid(3),
            grid(1),
            grid(3),
            grid(2),
            grid(1),
            grid(3),
            fold(2),
            fold(3),
            fold(1),
            fold(3),
            buf(2, 7, BY * 8, BLK),
            buf(2, 2, BY * 8, BLK),
            buf(2, 3, BY * 8, BLK),
            buf(2, 1, BY * 8, BLK),
            *pair(7, 8),
            *pair(3, 8),
            *pair(2, 16),
            *pair(3, 16),
            *pair(1, 16),
            *pair(3, 8),
            pltpu.SemaphoreType.DMA((copies,)),
            pltpu.SemaphoreType.DMA((copies,)),
            pltpu.SemaphoreType.DMA((2,)),
        ],
        compiler_params=pltpu.CompilerParams(
            collective_id=0, has_side_effects=True, vmem_limit_bytes=56 * 1024 * 1024
        ),
    )(
        pos,
        volume.reshape(BX, BY * BZ, BLK),
        dis,
        vel,
        acc,
        tile_own.reshape(TILES),
        tile_partner.reshape(TILES),
        tile_count,
        family_bits.reshape(TILES, WORDS, BLK),
        broken_bits.reshape(TILES, WORDS, BLK),
    )
    return tuple(v.reshape(3, BX, BY, BZ, BLK) for v in outs)


def solution(mesh):
    in_specs = (
        P(None, "gx", "gy", "gz", None),
        P("gx", "gy", "gz", None),
        P(None, "gx", "gy", "gz", None),
        P(None, "gx", "gy", "gz", None),
        P(None, "gx", "gy", "gz", None),
        P("gx", "gy", "gz", None),
        P("gx", "gy", "gz", None),
        P("gx", "gy", "gz"),
        P("gx", "gy", "gz", None, None, None),
        P("gx", "gy", "gz", None, None, None),
    )
    out_specs = (
        P(None, "gx", "gy", "gz", None),
        P(None, "gx", "gy", "gz", None),
        P(None, "gx", "gy", "gz", None),
    )
    return jax.shard_map(
        per_device, mesh=mesh, in_specs=in_specs, out_specs=out_specs, check_vma=False
    )
```

time: 587 us -> 110 us (0.19)
  the two profiles are of different devices: /device:TPU:392 before, /device:TPU:13 now
where the time goes in v1:
time: 110 us; the launch traced here: 109 us
  Pallas kernels  105 us (95%)
  local copies, waits for them, and re-layouts  2.87 us (3%)
  between operations  1.3 us (1%)
    pallas_call x1, Pallas kernels, per_device(): pl.pallas_call(kernel, out_shape=[out] * 3, in_specs=[vmem] * 5 + [smem]...  105 us
    unnamed x7, local copies, waits for them, and re-layouts  2.87 us

profile of v1, /device:TPU:13, one launch (start us, length us, event | category | flops | bytes accessed | tf_op | source)
XLA Modules:
  0.0 109.3 jit_solution(6423660287413968453)
XLA Ops:
  1.3 105.1 %shard_map.121 = (f32[3,4,8,128]{3,2,1,0:T(8,128)}, f32[3,4,8,128]{3,2,1,0:T(8,128)}, f32[3,4,8,128]{3,2,1,0:T(8,128)}) custom-call(f32[3,4,8,128]{3,2,1,0:T(8,128)} %bitcast.14, f32[4,8,128]{2,1,0:T(8,128)} %bitcast.21, f32[3,4,8,128]{3,2,1,0:T(8,128)} %bitcast.15, f32[3,4,8,128]{3,2,1,0:T(8,128)} %bitcast.16, f32[3,4,8,128]{3,2,1,0:T(8,128)} %bitcast.17, ...), custom_call_target="tpu_custom_call" | custom-call | tf_op jit(solution)/shard_map/pallas_call | solution.py:554
  106.4 0.0 copy-start.1
  106.4 1.4 %copy.17 = f32[3,4,4,2,128]{4,3,2,1,0:T(2,128)} copy(f32[3,4,4,2,128]{4,3,2,1,0:T(2,128)} %bitcast.20) | data formatting | bytes 98304
  107.8 0.0 copy-done.1
  107.8 0.0 copy-start
  107.8 0.6 copy.18
  108.5 0.2 copy-done
  108.7 0.6 copy.19
Async XLA Ops:
  106.4 1.4 %copy-start.1 = (f32[3,4,8,128]{3,2,1,0:T(8,128)S(1)}, f32[3,4,8,128]{3,2,1,0:T(8,128)}, u32[]{:S(2)}) copy-start(f32[3,4,8,128]{3,2,1,0:T(8,128)} %get-tuple-element.7) | copy-start | bytes 147460
  107.8 0.8 copy-start

commit v2 on v1

--- a/solution.py
+++ b/solution.py
@@ -17,7 +17,7 @@
 VOLUME_FLOOR = 2000.0
 TIME_DELTA = 0.05
 TINY = 1e-30
-UNROLL = 4
+UNROLL = 8
 ROWS = (BY + 2) * (BZ + 2) * 8
 
 YZ = [(-1, 0), (1, 0), (0, -1), (0, 1), (-1, -1), (-1, 1), (1, -1), (1, 1)]
@@ -72,7 +72,6 @@
     half,
     base,
     inv,
-    kap,
     w_ref,
     r_ref,
     e_ref,
@@ -83,18 +82,24 @@
     hot_t,
     hot,
     terms,
+    sum_m,
     sum_s1,
     sum_f1,
     sum_s2,
     sum_f2,
+    tot1,
+    tot2,
+    kapq,
     coef1,
     coef2,
     disp2,
+    fold_m,
     fold_s1,
     fold_f1,
     fold_s2,
     fold_f2,
     zs0,
+    zsm,
     zs1,
     zs2,
     zs3,
@@ -102,6 +107,8 @@
     xr0,
     xsb,
     xrb,
+    xsm,
+    xrm,
     xs1,
     xr1,
     xs2,
@@ -110,13 +117,25 @@
     xr3,
     xs4,
     xr4,
+    zf1,
+    yf1,
+    cf1,
+    zg1,
+    yg1,
+    cg1,
+    zf2,
+    yf2,
+    cf2,
+    zg2,
+    yg2,
+    cg2,
     send_sem,
     recv_sem,
     load_sem,
 ):
     gx, gy, gz = lax.axis_index("gx"), lax.axis_index("gy"), lax.axis_index("gz")
-    sent = []
     counter = [0]
+    pending = []
 
     def there(step):
         ok = None
@@ -134,7 +153,7 @@
             self.steps, self.base = steps, counter[0]
             counter[0] += len(steps)
             self.source, self.sink = source, sink
-            sent.append(self)
+            pending.append(self)
 
         def copy(self, i, step, back):
             opposite = tuple(-d for d in step)
@@ -159,7 +178,12 @@
             for i, step in enumerate(self.steps):
                 pl.when(there(step))(lambda i=i, step=step: self.copy(i, step, False).wait_send())
 
+    def settle():
+        while pending:
+            pending.pop(0).finish()
+
     yz_steps = [(0, dy, dz) for dy, dz in YZ]
+    diagonal_steps = [(dx, dy, dz) for dx in (-1, 1) for dy, dz in YZ]
     x_steps = [(-1, 0, 0), (1, 0, 0)]
 
     def fold_exchange(sums, fold):
@@ -169,7 +193,7 @@
             lambda s: fold.at[:, slot(s[1:])],
         )
 
-    def add_folds(sums, fold, channels):
+    def add_folds(dest, sums, fold, channels):
         for c in range(channels):
             for g in range(BY * BZ):
                 total = sums[c, column(g)]
@@ -177,26 +201,61 @@
                     if g in INNER[step]:
                         first = slot(step).start + INNER[step].index(g) * 8
                         total = total + fold[c, first : first + 8]
-                sums[c, column(g)] = total
-
-    def halo_exchange(array, packed, channels):
+                dest[c, column(g)] = total
+
+    def halo_exchange(array, packed, first, last):
         def source(s):
             step = s[1:]
             if step[0] == 0:
-                return packed.at[(step[1] + 1) // 2]
+                return packed.at[(step[1] + 1) // 2, first:last]
             groups = INNER[step]
-            return array.at[:, groups[0] * 8 : groups[-1] * 8 + 8]
+            return array.at[first:last, groups[0] * 8 : groups[-1] * 8 + 8]
 
         for side in (0, 1):
             for j in range(BY):
-                for c in range(channels):
+                for c in range(first, last):
                     packed[side, c, column(j)] = array[c, column(2 * j + side)]
-        return Exchange(yz_steps, source, lambda s: array.at[:, GHOST[s[1:]]])
-
-    def x_exchange(send, recv):
+        return Exchange(yz_steps, source, lambda s: array.at[first:last, GHOST[s[1:]]])
+
+    def x_exchange(send, recv, first, last):
         return Exchange(
-            x_steps, lambda s: send.at[(s[0] + 1) // 2], lambda s: recv.at[(s[0] + 1) // 2]
+            x_steps,
+            lambda s: send.at[(s[0] + 1) // 2, first:last],
+            lambda s: recv.at[(s[0] + 1) // 2, first:last],
         )
+
+    def diagonal_exchange(send, recv):
+        def of(buffers, s):
+            faces_z, faces_y, corners = buffers
+            x, y, z = ((d + 1) // 2 for d in s)
+            if s[1] == 0:
+                return faces_z.at[x, z]
+            return faces_y.at[x, y] if s[2] == 0 else corners.at[x, 2 * y + z]
+
+        return Exchange(diagonal_steps, lambda s: of(send, s), lambda s: of(recv, s))
+
+    def pack_diagonal(send, array):
+        faces_z, faces_y, corners = send
+        for side in (0, 1):
+            for j, x in enumerate(shared(side)):
+                for i in (0, 1):
+                    faces_z[side, i, j * 4 : j * 4 + 4] = array[0, pl.ds(8 * i + x, 4, stride=16), :]
+                    faces_y[side, i, j * 2 : j * 2 + 2] = array[0, pl.ds(48 * i + x, 2, stride=8), :]
+                for i, g in enumerate((0, 1, 6, 7)):
+                    corners[side, i, j : j + 1] = array[0, pl.ds(g * 8 + x, 1), :]
+
+    def add_diagonal(array, recv):
+        faces_z, faces_y, corners = recv
+        for side in (0, 1):
+            for j, x in enumerate(shared(side)):
+                for i, d in enumerate((-1, 1)):
+                    at = pl.ds(GHOST[(0, d)].start + x, 4, stride=8)
+                    array[0, at, :] = array[0, at, :] + faces_z[side, i, j * 4 : j * 4 + 4]
+                    at = pl.ds(GHOST[(d, 0)].start + x, 2, stride=8)
+                    array[0, at, :] = array[0, at, :] + faces_y[side, i, j * 2 : j * 2 + 2]
+                for i in range(4):
+                    at = pl.ds(GHOST[(i // 2 * 2 - 1, i % 2 * 2 - 1)].start + x, 1)
+                    array[0, at, :] = array[0, at, :] + corners[side, i, j : j + 1]
 
     def shared(side):
         return ((0, 1), (BX, BX + 1))[side]
@@ -215,7 +274,7 @@
 
     barrier = pltpu.get_barrier_semaphore()
     expected = jnp.int32(0)
-    for step in x_steps + yz_steps:
+    for step in x_steps + yz_steps + diagonal_steps:
         expected = expected + there(step).astype(jnp.int32)
 
         @pl.when(there(step))
@@ -233,41 +292,58 @@
         data[3, plane(x + 1), :] = vol[x]
         for k in range(3):
             data[k, plane(x + 1), :] = pos[k, x]
+    for side, x in ((0, 0), (1, BX - 1)):
+        xs0[side, 3] = vol[x]
+        for k in range(3):
+            xs0[side, k] = pos[k, x]
+    pl.semaphore_wait(barrier, expected)
+    xv = x_exchange(xs0, xr0, 0, 4)
+    xv.start()
+    for x in (0, BX - 1, 1, 2):
+        for k in range(3):
             h = vel[k, x] + 0.5 * TIME_DELTA * acc[k, x]
             u1 = dis[k, x] + TIME_DELTA * h
             data[4 + k, plane(x + 1), :] = u1
             half[k, x] = h
             base[k, plane(x + 1), :] = u1 + TIME_DELTA * h
-    for side, x in ((0, 1), (1, BX)):
-        for c in range(7):
-            xs0[side, c] = data[c, plane(x), :]
-        for c in range(3):
-            xsb[side, c] = base[c, plane(x), :]
-
-    pl.semaphore_wait(barrier, expected)
-    x0 = x_exchange(xs0, xr0)
-    xb = x_exchange(xsb, xrb)
-    x0.start()
+            if x == 0 or x == BX - 1:
+                xs0[x // (BX - 1), 4 + k] = u1
+                xsb[x // (BX - 1), k] = u1 + TIME_DELTA * h
+    xu = x_exchange(xs0, xr0, 4, 7)
+    xb = x_exchange(xsb, xrb, 0, 3)
+    xu.start()
 
     for side, step in enumerate(x_steps):
 
         @pl.when(jnp.logical_not(there(step)))
         def _(side=side):
-            for ref in (xr0, xrb, xr1, xr2, xr3, xr4):
+            for ref in (xr0, xrb, xrm, xr1, xr2, xr3, xr4):
                 ref[side] = jnp.zeros(ref.shape[1:], jnp.float32)
+
+    for step in diagonal_steps:
+
+        @pl.when(jnp.logical_not(there(step)))
+        def _(step=step):
+            x, y, z = ((d + 1) // 2 for d in step)
+            for faces_z, faces_y, corners in ((zg1, yg1, cg1), (zg2, yg2, cg2)):
+                if step[1] == 0:
+                    faces_z[x, z] = jnp.zeros((8, BLK), jnp.float32)
+                elif step[2] == 0:
+                    faces_y[x, y] = jnp.zeros((4, BLK), jnp.float32)
+                else:
+                    corners[x, 2 * y + z] = jnp.zeros((2, BLK), jnp.float32)
 
     for step in YZ:
 
         @pl.when(jnp.logical_not(there((0,) + step)))
         def _(step=step):
-            for ref in (data, coef1, disp2, coef2):
+            for ref in (data, kapq, disp2, tot1, tot2):
                 rows = GHOST[step]
                 ref[:, rows] = jnp.zeros((ref.shape[0], rows.stop - rows.start, BLK), jnp.float32)
-            for ref in (fold_s1, fold_f1, fold_s2, fold_f2):
+            for ref in (fold_m, fold_s1, fold_f1, fold_s2, fold_f2):
                 rows = slot(step)
                 ref[:, rows] = jnp.zeros((ref.shape[0], rows.stop - rows.start, BLK), jnp.float32)
 
-    terms[...] = jnp.zeros_like(terms)
     hot_t[...] = jnp.zeros_like(hot_t)
     org = [g.astype(jnp.float32) * 16.0 for g in (gx, gy, gz)]
     load_f.wait()
@@ -307,7 +383,7 @@
             )
         return carry
 
-    lax.fori_loop(0, TILES, mask_body, 0, unroll=UNROLL)
+    lax.fori_loop(0, TILES, mask_body, 0, unroll=4)
     picked = jnp.concatenate([hot_t[0].T, hot_t[1].T], axis=0)[0:ROWS].astype(jnp.bfloat16)
     hot[:, 0:128] = picked
     hot[:, 128:256] = picked
@@ -323,49 +399,62 @@
                     )
             return carry
 
-        lax.fori_loop(0, BY * BZ, body, 0)
+        lax.fori_loop(0, BY * BZ, body, 0, unroll=4)
 
     put_columns(
         col_x, 0, lambda rows: [data[k, rows, :] - org[k] for k in range(3)] + [data[3, rows, :]]
     )
+
+    def place_x(first, last):
+        for side, x in ((0, 0), (1, BX + 1)):
+            for c in range(first, last):
+                data[c, plane(x), :] = xr0[side, c]
+
+    xv.arrive()
+    place_x(0, 4)
+    hv = halo_exchange(data, zs0, 0, 4)
+    hv.start()
     put_columns(
         col_y,
         0,
         lambda rows: [(data[k, rows, :] - org[k]) + data[4 + k, rows, :] for k in range(3)],
     )
-
-    x0.arrive()
-    for side, x in ((0, 0), (1, BX + 1)):
-        for c in range(7):
-            data[c, plane(x), :] = xr0[side, c]
-    h0 = halo_exchange(data, zs0, 7)
-    h0.start()
-    xb.start()
+    xu.arrive()
+    place_x(4, 7)
+    hu = halo_exchange(data, zs0, 4, 7)
+    hu.start()
     volume = data[3, 0:OWN_ROWS]
     inv[...] = jnp.where(volume > 0.0, 1.0 / jnp.where(volume > 0.0, volume, 1.0), 0.0)
-    h0.arrive()
+    hv.arrive()
     for k in range(3):
         xrel[k] = data[k] - org[k]
-        ypos[k] = xrel[k] + data[4 + k]
+    xrel[3] = data[3]
 
     def far_row(ref, k, at):
         return ref[k, pl.ds(at, 1), :]
 
-    diagonal = sub == lane
-
     def put_sums(t, c, values, far_sign=1):
-        per_a = jnp.sum(values, axis=1, keepdims=True)
-        near = jnp.sum(jnp.where(diagonal, per_a, 0.0), axis=0, keepdims=True)
-        far = jnp.sum(values, axis=0, keepdims=True)
-        terms[c, pl.ds(2 * t, 1), :] = near
-        terms[c, pl.ds(2 * t + 1, 1), :] = far if far_sign > 0 else -far
+        near = jnp.sum(values.T.reshape(16, 8, BLK), axis=0)
+        far = jnp.sum(values.reshape(16, 8, BLK), axis=0)
+        first = pl.multiple_of(t * 16, 16)
+        terms[c, pl.ds(first, 8), :] = near
+        terms[c, pl.ds(first + 8, 8), :] = far if far_sign > 0 else -far
 
     def gather_sums(sums, channels):
-        full = jnp.concatenate([terms[c] for c in range(channels)], axis=1)
+        added = []
+        for c in range(channels):
+            total = terms[c, pl.ds(0, 2 * TILES, stride=8), :]
+            for q in range(1, 8):
+                total = total + terms[c, pl.ds(q, 2 * TILES, stride=8), :]
+            added.append(total)
+        full = jnp.concatenate(added, axis=1)
         high = full.astype(jnp.bfloat16)
         low = (full - high.astype(jnp.float32)).astype(jnp.bfloat16)
+        rest = jnp.zeros((128 - 2 * TILES, channels * 128), jnp.bfloat16)
         out = jnp.dot(
-            hot[...], jnp.concatenate([high, low], axis=0), preferred_element_type=jnp.float32
+            hot[...],
+            jnp.concatenate([high, rest, low, rest], axis=0),
+            preferred_element_type=jnp.float32,
         )
         for c in range(channels):
             sums[c] = out[:, c * 128 : (c + 1) * 128]
@@ -376,18 +465,15 @@
         inverse = lax.rsqrt(square)
         return d, square * inverse, inverse
 
-    def first_body(t, carry):
+    def rest_body(t, carry):
         near, at = near_at[t], far_at[t]
         o = [far_row(xrel, k, at) - col_x[near, k] for k in range(3)]
         square = jnp.maximum(o[0] * o[0] + o[1] * o[1] + o[2] * o[2], TINY)
         rest = square * lax.rsqrt(square)
-        weight = w_ref[t] * (col_x[near, 3] * far_row(data, 3, at))
+        weight = w_ref[t] * (col_x[near, 3] * far_row(xrel, 3, at))
         w_ref[t] = weight
         r_ref[t] = rest
-        weighted = weight * rest
-        put_sums(t, 1, weighted * rest)
-        _, length, _ = deformed(near, at)
-        put_sums(t, 0, weighted * (length - rest))
+        put_sums(t, 0, weight * rest * rest)
         return carry
 
     def sum_body(t, carry):
@@ -409,7 +495,7 @@
     def force_body(far_p, t, carry):
         near, at = near_at[t], far_at[t]
         c = r_ref[t] * (col_c[near, 0] + far_row(far_p, 0, at))
-        c = c + e_ref[t] * (col_c[near, 1] + far_row(coef1, 1, at))
+        c = c + e_ref[t] * (col_c[near, 1] + far_row(kapq, 1, at))
         for k in range(3):
             put_sums(t, k, c * n_ref[t, k], far_sign=-1)
         return carry
@@ -417,49 +503,91 @@
     def tiles(body):
         lax.fori_loop(0, TILES, body, 0, unroll=UNROLL)
 
-    own_rows = slice(0, OWN_ROWS)
-
-    tiles(first_body)
-    gather_sums(sum_s1, 2)
-    f = fold_exchange(sum_s1, fold_s1)
-    f.start()
-    f.arrive()
-    add_folds(sum_s1, fold_s1, 2)
-    pack_x(xs1, sum_s1, 2)
-    x1 = x_exchange(xs1, xr1)
-    x1.start()
+    own_rows, ghost_rows = slice(0, OWN_ROWS), slice(OWN_ROWS, ROWS)
+
+    def total_of(tot, sums, fold, fold_way, buffers, packed, xs, xr):
+        send, recv = buffers
+        fold_way.arrive()
+        add_folds(tot, sums, fold, 1)
+        pack_x(xs, tot, 1)
+        main = x_exchange(xs, xr, 0, 1)
+        main.start()
+        pack_diagonal(send, tot)
+        diagonal = diagonal_exchange(send, recv)
+        diagonal.start()
+        halo = halo_exchange(tot, packed, 0, 1)
+        halo.start()
+        return main, diagonal, halo
+
+    tiles(rest_body)
+    gather_sums(sum_m, 1)
+    fm = fold_exchange(sum_m, fold_m)
+    fm.start()
+    hu.arrive()
+    for k in range(3):
+        ypos[k] = xrel[k] + data[4 + k]
+    tiles(sum_body)
+    gather_sums(sum_s1, 1)
+    fs = fold_exchange(sum_s1, fold_s1)
+    fs.start()
+    fm.arrive()
+    add_folds(sum_m, sum_m, fold_m, 1)
+    pack_x(xsm, sum_m, 1)
+    xm = x_exchange(xsm, xrm, 0, 1)
+    xm.start()
+    buffers = ((zf1, yf1, cf1), (zg1, yg1, cg1))
+    main, diagonal, halo = total_of(tot1, sum_s1, fold_s1, fs, buffers, zs1, xs1, xr1)
     tiles(geometry_body)
-    x1.arrive()
-    add_x(sum_s1, xr1, 2)
-    floored = jnp.maximum(sum_s1[1, own_rows] * inv[...], VOLUME_FLOOR)
-    kap[...] = (3.0 * (3.0 * K_BULK - 5.0 * MU_SHEAR)) * inv[...] / floored / floored
-    coef1[0, own_rows] = sum_s1[0, own_rows] * kap[...]
-    coef1[1, own_rows] = 15.0 * MU_SHEAR / floored
-    h1 = halo_exchange(coef1, zs1, 2)
-    h1.start()
-    put_columns(col_c, 0, lambda rows: [coef1[k, rows, :] for k in range(2)])
-    h1.arrive()
+    xm.arrive()
+    add_x(sum_m, xrm, 1)
+    floored = jnp.maximum(sum_m[0, own_rows] * inv[...], VOLUME_FLOOR)
+    kapq[0, own_rows] = (3.0 * (3.0 * K_BULK - 5.0 * MU_SHEAR)) * inv[...] / floored / floored
+    kapq[1, own_rows] = 15.0 * MU_SHEAR / floored
+    hm = halo_exchange(kapq, zsm, 0, 2)
+    hm.start()
+    put_columns(col_c, 1, lambda rows: [kapq[1, rows, :]])
+
+    def finish_total(tot, way, recv, coef, xr, kapq_halo=None):
+        main, diagonal, halo = way
+        main.arrive()
+        halo.finish()
+        pending.remove(halo)
+        add_x(tot, xr, 1)
+        coef[0, own_rows] = tot[0, own_rows] * kapq[0, own_rows]
+        put_columns(col_c, 0, lambda rows: [coef[0, rows, :]])
+        halo.arrive()
+        diagonal.arrive()
+        add_diagonal(tot, recv)
+        if kapq_halo is not None:
+            kapq_halo.arrive()
+        coef[0, ghost_rows] = tot[0, ghost_rows] * kapq[0, ghost_rows]
+
+    finish_total(tot1, (main, diagonal, halo), buffers[1], coef1, xr1, hm)
+    xb.start()
 
     tiles(functools.partial(force_body, coef1))
     gather_sums(sum_f1, 3)
     f = fold_exchange(sum_f1, fold_f1)
     f.start()
+    f.arrive()
+    add_folds(sum_f1, sum_f1, fold_f1, 3)
+    pack_x(xs2, sum_f1, 3)
+    x2 = x_exchange(xs2, xr2, 0, 3)
+    x2.start()
     xb.arrive()
     for side, x in ((0, 0), (1, BX + 1)):
         for k in range(3):
             base[k, plane(x), :] = xrb[side, k]
-    f.arrive()
-    add_folds(sum_f1, fold_f1, 3)
-    pack_x(xs2, sum_f1, 3)
-    x2 = x_exchange(xs2, xr2)
-    x2.start()
+    pending.remove(x2)
+    settle()
+    pending.append(x2)
     x2.arrive()
     add_x(sum_f1, xr2, 3)
     for k in range(3):
         force = sum_f1[k, own_rows] * inv[...]
         sum_f1[k, own_rows] = force
         disp2[k, own_rows] = base[k] + (TIME_DELTA * TIME_DELTA) * force
-    h2 = halo_exchange(disp2, zs2, 3)
+    h2 = halo_exchange(disp2, zs2, 0, 3)
     h2.start()
     put_columns(
         col_y, 0, lambda rows: [xrel[k, rows, :] + disp2[k, rows, :] for k in range(3)]
@@ -473,36 +601,30 @@
 
     tiles(sum_body)
     gather_sums(sum_s2, 1)
-    f = fold_exchange(sum_s2, fold_s2)
-    f.start()
-    f.arrive()
-    add_folds(sum_s2, fold_s2, 1)
-    pack_x(xs3, sum_s2, 1)
-    x3 = x_exchange(xs3, xr3)
-    x3.start()
+    fs = fold_exchange(sum_s2, fold_s2)
+    fs.start()
+    buffers = ((zf2, yf2, cf2), (zg2, yg2, cg2))
+    way = total_of(tot2, sum_s2, fold_s2, fs, buffers, zs3, xs3, xr3)
     tiles(geometry_body)
-    x3.arrive()
-    add_x(sum_s2, xr3, 1)
-    coef2[0, own_rows] = sum_s2[0, own_rows] * kap[...]
-    h3 = halo_exchange(coef2, zs3, 1)
-    h3.start()
-    put_columns(col_c, 0, lambda rows: [coef2[0, rows, :]])
-    h3.arrive()
+    finish_total(tot2, way, buffers[1], coef2, xr3)
 
     tiles(functools.partial(force_body, coef2))
     gather_sums(sum_f2, 3)
     f = fold_exchange(sum_f2, fold_f2)
     f.start()
     f.arrive()
-    add_folds(sum_f2, fold_f2, 3)
+    add_folds(sum_f2, sum_f2, fold_f2, 3)
     for side, x in ((0, 0), (1, BX + 1)):
         for k in range(3):
             xs4[side, k] = sum_f2[k, plane(x), :]
-    x4 = x_exchange(xs4, xr4)
+    x4 = x_exchange(xs4, xr4, 0, 3)
     x4.start()
+    pending.remove(x4)
+    out_v[...] = half[...]
     for x in range(BX):
         for k in range(3):
             out_u[k, x] = disp2[k, plane(x + 1), :]
+    settle()
     x4.arrive()
     for x in range(BX):
         for k in range(3):
@@ -513,9 +635,13 @@
                 force = force + xr4[1, k]
             force = force * inv[plane(x + 1), :]
             out_a[k, x] = force
-            out_v[k, x] = half[k, x] + 0.5 * TIME_DELTA * force
-    for exchange in sent:
-        exchange.finish()
+    x4.finish()
+
+
+def finish_kernel(u, h, a, out_u, out_v, out_a):
+    out_u[...] = u[...]
+    out_v[...] = h[...] + 0.5 * TIME_DELTA * a[...]
+    out_a[...] = a[...]
 
 
 def per_device(
@@ -547,8 +673,11 @@
     def pair(channels, rows):
         return [buf(2, channels, rows, BLK), buf(2, channels, rows, BLK)]
 
+    def diagonals():
+        return [buf(2, 2, 8, BLK), buf(2, 2, 4, BLK), buf(2, 4, 2, BLK)]
+
     bits = pltpu.VMEM((TILES, WORDS, BLK), jnp.int32)
-    copies = 8 * len(YZ) + 6 * 2
+    copies = 11 * len(YZ) + 8 * 2 + 2 * 16
     values = (positions, displacement, velocity, acceleration)
     pos, dis, vel, acc = (v.reshape(3, BX, BY * BZ, BLK) for v in values)
     outs = pl.pallas_call(
@@ -562,11 +691,10 @@
             pltpu.SMEM((TILES,), jnp.int32),
             pltpu.SMEM((TILES,), jnp.int32),
             grid(7),
-            grid(3),
+            grid(4),
             grid(3),
             buf(3, BX, BY * BZ, BLK),
             buf(3, OWN_ROWS, BLK),
-            buf(OWN_ROWS, BLK),
             buf(OWN_ROWS, BLK),
             buf(TILES, BLK, BLK),
             buf(TILES, BLK, BLK),
@@ -577,28 +705,39 @@
             buf(BX * BY * BZ, 2, BLK, BLK),
             buf(2, 128, 128),
             buf(ROWS, 256, dtype=jnp.bfloat16),
-            buf(3, 128, 128),
-            grid(2),
+            buf(3, TILES * 16, 128),
+            grid(1),
+            grid(1),
             grid(3),
             grid(1),
             grid(3),
+            grid(1),
+            grid(1),
             grid(2),
             grid(1),
+            grid(1),
             grid(3),
-            fold(2),
+            fold(1),
+            fold(1),
             fold(3),
             fold(1),
             fold(3),
             buf(2, 7, BY * 8, BLK),
             buf(2, 2, BY * 8, BLK),
+            buf(2, 1, BY * 8, BLK),
             buf(2, 3, BY * 8, BLK),
             buf(2, 1, BY * 8, BLK),
             *pair(7, 8),
             *pair(3, 8),
-            *pair(2, 16),
+            *pair(1, 16),
+            *pair(1, 16),
             *pair(3, 16),
             *pair(1, 16),
             *pair(3, 8),
+            *diagonals(),
+            *diagonals(),
+            *diagonals(),
+            *diagonals(),
             pltpu.SemaphoreType.DMA((copies,)),
             pltpu.SemaphoreType.DMA((copies,)),
             pltpu.SemaphoreType.DMA((2,)),
@@ -618,6 +757,9 @@
         family_bits.reshape(TILES, WORDS, BLK),
         broken_bits.reshape(TILES, WORDS, BLK),
     )
+    outs = pl.pallas_call(
+        finish_kernel, out_shape=[out] * 3, in_specs=[vmem] * 3, out_specs=[vmem] * 3
+    )(*outs)
     return tuple(v.reshape(3, BX, BY, BZ, BLK) for v in outs)
 
 

time: 110 us -> 101 us (0.918)
  the two profiles are of different devices: /device:TPU:13 before, /device:TPU:71 now
where the time goes in v2:
time: 101 us
  Pallas kernels  99.3 us (98%)
  between operations  1.29 us (1%)
    pallas_call x1, Pallas kernels, per_device(): pl.pallas_call(kernel, out_shape=[out] * 3, in_specs=[vmem] * 5 + [smem]...  97.8 us

profile of v2, /device:TPU:71, one launch (start us, length us, event | category | flops | bytes accessed | tf_op | source)
XLA Modules:
  0.0 100.6 jit_solution(5045206953795694410)
XLA Ops:
  1.3 97.8 %shard_map.121 = (f32[3,4,8,128]{3,2,1,0:T(8,128)}, f32[3,4,8,128]{3,2,1,0:T(8,128)}, f32[3,4,8,128]{3,2,1,0:T(8,128)}) custom-call(f32[3,4,8,128]{3,2,1,0:T(8,128)} %bitcast.14, f32[4,8,128]{2,1,0:T(8,128)} %bitcast.18, f32[3,4,8,128]{3,2,1,0:T(8,128)} %bitcast.15, f32[3,4,8,128]{3,2,1,0:T(8,128)} %bitcast.16, f32[3,4,8,128]{3,2,1,0:T(8,128)} %bitcast.17, ...), custom_call_target="tpu_custom_call" | custom-call | tf_op jit(solution)/shard_map/pallas_call | solution.py:683
  99.1 1.5 %shard_map.122 = (f32[3,4,8,128]{3,2,1,0:T(8,128)}, f32[3,4,8,128]{3,2,1,0:T(8,128)}, f32[3,4,8,128]{3,2,1,0:T(8,128)}) custom-call(f32[3,4,8,128]{3,2,1,0:T(8,128)} %get-tuple-element.9.u, f32[3,4,8,128]{3,2,1,0:T(8,128)} %get-tuple-element.10.h, f32[3,4,8,128]{3,2,1,0:T(8,128)} %get-tuple-element.11.a), custom_call_target="tpu_custom_call" | custom-call | tf_op jit(solution)/shard_map/pallas_call | solution.py:760

commit v3 on v2

--- a/solution.py
+++ b/solution.py
@@ -49,16 +49,24 @@
 
 
 def kernel(
+    pos_hbm,
+    vol_hbm,
+    dis_hbm,
+    vel_hbm,
+    acc_hbm,
+    own,
+    par,
+    cnt,
+    fam_hbm,
+    brk_hbm,
+    u_hbm,
+    v_hbm,
+    a_hbm,
     pos,
     vol,
     dis,
     vel,
     acc,
-    own,
-    par,
-    cnt,
-    fam_hbm,
-    brk_hbm,
     out_u,
     out_v,
     out_a,
@@ -129,6 +137,12 @@
     zg2,
     yg2,
     cg2,
+    zf4,
+    yf4,
+    cf4,
+    zg4,
+    yg4,
+    cg4,
     send_sem,
     recv_sem,
     load_sem,
@@ -283,15 +297,25 @@
                 barrier, inc=1, device_id=target(step), device_id_type=pl.DeviceIdType.MESH
             )
 
-    load_f = pltpu.make_async_copy(fam_hbm, fam, load_sem.at[0])
-    load_b = pltpu.make_async_copy(brk_hbm, brk, load_sem.at[1])
-    load_f.start()
-    load_b.start()
-
-    for x in range(BX):
-        data[3, plane(x + 1), :] = vol[x]
-        for k in range(3):
-            data[k, plane(x + 1), :] = pos[k, x]
+    pairs = (
+        (pos_hbm, pos),
+        (vol_hbm, vol),
+        (dis_hbm, dis),
+        (vel_hbm, vel),
+        (acc_hbm, acc),
+        (fam_hbm, fam),
+        (brk_hbm, brk),
+        (out_u, u_hbm),
+        (out_v, v_hbm),
+        (out_a, a_hbm),
+    )
+    moves = [pltpu.make_async_copy(a, b, load_sem.at[i]) for i, (a, b) in enumerate(pairs)]
+    loads, stores = moves[:7], moves[7:]
+    for load in loads:
+        load.start()
+
+    loads[0].wait()
+    loads[1].wait()
     for side, x in ((0, 0), (1, BX - 1)):
         xs0[side, 3] = vol[x]
         for k in range(3):
@@ -299,6 +323,8 @@
     pl.semaphore_wait(barrier, expected)
     xv = x_exchange(xs0, xr0, 0, 4)
     xv.start()
+    for load in loads[2:5]:
+        load.wait()
     for x in (0, BX - 1, 1, 2):
         for k in range(3):
             h = vel[k, x] + 0.5 * TIME_DELTA * acc[k, x]
@@ -312,6 +338,10 @@
     xu = x_exchange(xs0, xr0, 4, 7)
     xb = x_exchange(xsb, xrb, 0, 3)
     xu.start()
+    for x in range(BX):
+        data[3, plane(x + 1), :] = vol[x]
+        for k in range(3):
+            data[k, plane(x + 1), :] = pos[k, x]
 
     for side, step in enumerate(x_steps):
 
@@ -332,6 +362,12 @@
                     faces_y[x, y] = jnp.zeros((4, BLK), jnp.float32)
                 else:
                     corners[x, 2 * y + z] = jnp.zeros((2, BLK), jnp.float32)
+            if step[1] == 0:
+                zg4[x, z] = jnp.zeros((3, 4, BLK), jnp.float32)
+            elif step[2] == 0:
+                yg4[x, y] = jnp.zeros((3, 2, BLK), jnp.float32)
+            else:
+                cg4[x, 2 * y + z] = jnp.zeros((3, 1, BLK), jnp.float32)
 
     for step in YZ:
 
@@ -346,8 +382,8 @@
 
     hot_t[...] = jnp.zeros_like(hot_t)
     org = [g.astype(jnp.float32) * 16.0 for g in (gx, gy, gz)]
-    load_f.wait()
-    load_b.wait()
+    loads[5].wait()
+    loads[6].wait()
     sub = lax.broadcasted_iota(jnp.int32, (BLK, BLK), 0)
     lane = lax.broadcasted_iota(jnp.int32, (BLK, BLK), 1)
 
@@ -610,22 +646,48 @@
 
     tiles(functools.partial(force_body, coef2))
     gather_sums(sum_f2, 3)
-    f = fold_exchange(sum_f2, fold_f2)
-    f.start()
-    f.arrive()
-    add_folds(sum_f2, sum_f2, fold_f2, 3)
     for side, x in ((0, 0), (1, BX + 1)):
         for k in range(3):
             xs4[side, k] = sum_f2[k, plane(x), :]
     x4 = x_exchange(xs4, xr4, 0, 3)
     x4.start()
-    pending.remove(x4)
+    for side, x in ((0, 0), (1, BX + 1)):
+        for k in range(3):
+            for i, d in enumerate((-1, 1)):
+                at = pl.ds(GHOST[(0, d)].start + x, 4, stride=8)
+                zf4[side, i, k] = sum_f2[k, at, :]
+                at = pl.ds(GHOST[(d, 0)].start + x, 2, stride=8)
+                yf4[side, i, k] = sum_f2[k, at, :]
+            for i in range(4):
+                at = pl.ds(GHOST[(i // 2 * 2 - 1, i % 2 * 2 - 1)].start + x, 1)
+                cf4[side, i, k] = sum_f2[k, at, :]
+    d4 = diagonal_exchange((zf4, yf4, cf4), (zg4, yg4, cg4))
+    d4.start()
+    f = fold_exchange(sum_f2, fold_f2)
+    f.start()
+    for way in (x4, d4, f):
+        pending.remove(way)
     out_v[...] = half[...]
     for x in range(BX):
         for k in range(3):
             out_u[k, x] = disp2[k, plane(x + 1), :]
+    stores[0].start()
+    stores[1].start()
     settle()
+    f.arrive()
+    add_folds(sum_f2, sum_f2, fold_f2, 3)
     x4.arrive()
+    d4.arrive()
+    for side, x in ((0, 1), (1, BX)):
+        for k in range(3):
+            for i in (0, 1):
+                at = pl.ds(8 * i + x, 4, stride=16)
+                sum_f2[k, at, :] = sum_f2[k, at, :] + zg4[side, i, k]
+                at = pl.ds(48 * i + x, 2, stride=8)
+                sum_f2[k, at, :] = sum_f2[k, at, :] + yg4[side, i, k]
+            for i, g in enumerate((0, 1, 6, 7)):
+                at = pl.ds(g * 8 + x, 1)
+                sum_f2[k, at, :] = sum_f2[k, at, :] + cg4[side, i, k]
     for x in range(BX):
         for k in range(3):
             force = sum_f2[k, plane(x + 1), :]
@@ -633,9 +695,12 @@
                 force = force + xr4[0, k]
             if x == BX - 1:
                 force = force + xr4[1, k]
-            force = force * inv[plane(x + 1), :]
-            out_a[k, x] = force
-    x4.finish()
+            out_a[k, x] = force * inv[plane(x + 1), :]
+    stores[2].start()
+    for way in (x4, d4, f):
+        way.finish()
+    for store in stores:
+        store.wait()
 
 
 def finish_kernel(u, h, a, out_u, out_v, out_a):
@@ -676,16 +741,23 @@
     def diagonals():
         return [buf(2, 2, 8, BLK), buf(2, 2, 4, BLK), buf(2, 4, 2, BLK)]
 
+    def last_diagonals():
+        return [buf(2, 2, 3, 4, BLK), buf(2, 2, 3, 2, BLK), buf(2, 4, 3, 1, BLK)]
+
     bits = pltpu.VMEM((TILES, WORDS, BLK), jnp.int32)
-    copies = 11 * len(YZ) + 8 * 2 + 2 * 16
+    copies = 11 * len(YZ) + 8 * 2 + 3 * 16
+    points = buf(3, BX, BY * BZ, BLK)
     values = (positions, displacement, velocity, acceleration)
     pos, dis, vel, acc = (v.reshape(3, BX, BY * BZ, BLK) for v in values)
     outs = pl.pallas_call(
         kernel,
         out_shape=[out] * 3,
-        in_specs=[vmem] * 5 + [smem] * 3 + [hbm] * 2,
-        out_specs=[vmem] * 3,
+        in_specs=[hbm] * 5 + [smem] * 3 + [hbm] * 2,
+        out_specs=[hbm] * 3,
         scratch_shapes=[
+            points,
+            buf(BX, BY * BZ, BLK),
+            *[points] * 6,
             bits,
             bits,
             pltpu.SMEM((TILES,), jnp.int32),
@@ -738,9 +810,11 @@
             *diagonals(),
             *diagonals(),
             *diagonals(),
+            *last_diagonals(),
+            *last_diagonals(),
             pltpu.SemaphoreType.DMA((copies,)),
             pltpu.SemaphoreType.DMA((copies,)),
-            pltpu.SemaphoreType.DMA((2,)),
+            pltpu.SemaphoreType.DMA((10,)),
         ],
         compiler_params=pltpu.CompilerParams(
             collective_id=0, has_side_effects=True, vmem_limit_bytes=56 * 1024 * 1024

time: 101 us -> 101 us (level)
  the two profiles are of different devices: /device:TPU:71 before, /device:TPU:103 now
where the time goes in v3:
time: 101 us
  Pallas kernels  99.7 us (99%)
  between operations  1.29 us (1%)
    pallas_call x1, Pallas kernels, per_device(): pl.pallas_call(kernel, out_shape=[out] * 3, in_specs=[hbm] * 5 + [smem] *...  98.2 us

profile of v3, /device:TPU:103, one launch (start us, length us, event | category | flops | bytes accessed | tf_op | source)
XLA Modules:
  0.0 101.0 jit_solution(17667859609189714220)
XLA Ops:
  1.3 98.2 %shard_map.121 = (f32[3,4,8,128]{3,2,1,0:T(8,128)}, f32[3,4,8,128]{3,2,1,0:T(8,128)}, f32[3,4,8,128]{3,2,1,0:T(8,128)}) custom-call(f32[3,4,8,128]{3,2,1,0:T(8,128)} %bitcast.14, f32[4,8,128]{2,1,0:T(8,128)} %bitcast.18, f32[3,4,8,128]{3,2,1,0:T(8,128)} %bitcast.15, f32[3,4,8,128]{3,2,1,0:T(8,128)} %bitcast.16, f32[3,4,8,128]{3,2,1,0:T(8,128)} %bitcast.17, ...), custom_call_target="tpu_custom_call" | custom-call | tf_op jit(solution)/shard_map/pallas_call | solution.py:752
  99.5 1.5 %shard_map.122 = (f32[3,4,8,128]{3,2,1,0:T(8,128)}, f32[3,4,8,128]{3,2,1,0:T(8,128)}, f32[3,4,8,128]{3,2,1,0:T(8,128)}) custom-call(f32[3,4,8,128]{3,2,1,0:T(8,128)} %get-tuple-element.9.u, f32[3,4,8,128]{3,2,1,0:T(8,128)} %get-tuple-element.10.h, f32[3,4,8,128]{3,2,1,0:T(8,128)} %get-tuple-element.11.a), custom_call_target="tpu_custom_call" | custom-call | tf_op jit(solution)/shard_map/pallas_call | solution.py:834

commit v4 on v3

--- a/solution.py
+++ b/solution.py
@@ -82,6 +82,7 @@
     inv,
     w_ref,
     r_ref,
+    wr_ref,
     e_ref,
     n_ref,
     col_x,
@@ -288,15 +289,17 @@
 
     barrier = pltpu.get_barrier_semaphore()
     expected = jnp.int32(0)
-    for step in x_steps + yz_steps + diagonal_steps:
-        expected = expected + there(step).astype(jnp.int32)
-
-        @pl.when(there(step))
-        def _(step=step):
-            pl.semaphore_signal(
-                barrier, inc=1, device_id=target(step), device_id_type=pl.DeviceIdType.MESH
-            )
-
+
+    def greet(steps):
+        for step in steps:
+
+            @pl.when(there(step))
+            def _(step=step):
+                pl.semaphore_signal(
+                    barrier, inc=1, device_id=target(step), device_id_type=pl.DeviceIdType.MESH
+                )
+
+    greet(x_steps)
     pairs = (
         (pos_hbm, pos),
         (vol_hbm, vol),
@@ -313,6 +316,10 @@
     loads, stores = moves[:7], moves[7:]
     for load in loads:
         load.start()
+    greet(diagonal_steps + yz_steps)
+    for step in x_steps + yz_steps + diagonal_steps:
+        expected = expected + there(step).astype(jnp.int32)
+
 
     loads[0].wait()
     loads[1].wait()
@@ -509,29 +516,36 @@
         weight = w_ref[t] * (col_x[near, 3] * far_row(xrel, 3, at))
         w_ref[t] = weight
         r_ref[t] = rest
-        put_sums(t, 0, weight * rest * rest)
+        weighted = weight * rest
+        wr_ref[t] = weighted
+        put_sums(t, 0, weighted * rest)
         return carry
 
     def sum_body(t, carry):
         near, at = near_at[t], far_at[t]
         _, length, _ = deformed(near, at)
-        rest = r_ref[t]
-        put_sums(t, 0, w_ref[t] * rest * (length - rest))
+        put_sums(t, 0, wr_ref[t] * (length - r_ref[t]))
         return carry
 
-    def geometry_body(t, carry):
+    def geometry_body(known_q, t, carry):
         near, at = near_at[t], far_at[t]
         d, length, inverse = deformed(near, at)
-        e_ref[t] = length - r_ref[t]
+        extension = length - r_ref[t]
+        if known_q:
+            extension = extension * (col_c[near, 1] + far_row(kapq, 1, at))
+        e_ref[t] = extension
         scale = w_ref[t] * inverse
         for k in range(3):
             n_ref[t, k] = scale * d[k]
         return carry
 
-    def force_body(far_p, t, carry):
+    def force_body(far_p, known_q, t, carry):
         near, at = near_at[t], far_at[t]
         c = r_ref[t] * (col_c[near, 0] + far_row(far_p, 0, at))
-        c = c + e_ref[t] * (col_c[near, 1] + far_row(kapq, 1, at))
+        if known_q:
+            c = c + e_ref[t]
+        else:
+            c = c + e_ref[t] * (col_c[near, 1] + far_row(kapq, 1, at))
         for k in range(3):
             put_sums(t, k, c * n_ref[t, k], far_sign=-1)
         return carry
@@ -573,7 +587,7 @@
     xm.start()
     buffers = ((zf1, yf1, cf1), (zg1, yg1, cg1))
     main, diagonal, halo = total_of(tot1, sum_s1, fold_s1, fs, buffers, zs1, xs1, xr1)
-    tiles(geometry_body)
+    tiles(functools.partial(geometry_body, False))
     xm.arrive()
     add_x(sum_m, xrm, 1)
     floored = jnp.maximum(sum_m[0, own_rows] * inv[...], VOLUME_FLOOR)
@@ -601,7 +615,7 @@
     finish_total(tot1, (main, diagonal, halo), buffers[1], coef1, xr1, hm)
     xb.start()
 
-    tiles(functools.partial(force_body, coef1))
+    tiles(functools.partial(force_body, coef1, False))
     gather_sums(sum_f1, 3)
     f = fold_exchange(sum_f1, fold_f1)
     f.start()
@@ -641,10 +655,10 @@
     fs.start()
     buffers = ((zf2, yf2, cf2), (zg2, yg2, cg2))
     way = total_of(tot2, sum_s2, fold_s2, fs, buffers, zs3, xs3, xr3)
-    tiles(geometry_body)
+    tiles(functools.partial(geometry_body, True))
     finish_total(tot2, way, buffers[1], coef2, xr3)
 
-    tiles(functools.partial(force_body, coef2))
+    tiles(functools.partial(force_body, coef2, True))
     gather_sums(sum_f2, 3)
     for side, x in ((0, 0), (1, BX + 1)):
         for k in range(3):
@@ -768,6 +782,7 @@
             buf(3, BX, BY * BZ, BLK),
             buf(3, OWN_ROWS, BLK),
             buf(OWN_ROWS, BLK),
+            buf(TILES, BLK, BLK),
             buf(TILES, BLK, BLK),
             buf(TILES, BLK, BLK),
             buf(TILES, BLK, BLK),

time: 101 us -> 101 us (level)
  the two profiles are of different devices: /device:TPU:103 before, /device:TPU:111 now
where the time goes in v4:
time: 101 us; the launch traced here: 99.7 us
  Pallas kernels  98.4 us (97%)
  between operations  1.29 us (1%)
    pallas_call x1, Pallas kernels, per_device(): pl.pallas_call(kernel, out_shape=[out] * 3, in_specs=[hbm] * 5 + [smem] *...  96.9 us

profile of v4, /device:TPU:111, one launch (start us, length us, event | category | flops | bytes accessed | tf_op | source)
XLA Modules:
  0.0 99.7 jit_solution(6699469480519098853)
XLA Ops:
  1.3 96.9 %shard_map.121 = (f32[3,4,8,128]{3,2,1,0:T(8,128)}, f32[3,4,8,128]{3,2,1,0:T(8,128)}, f32[3,4,8,128]{3,2,1,0:T(8,128)}) custom-call(f32[3,4,8,128]{3,2,1,0:T(8,128)} %bitcast.14, f32[4,8,128]{2,1,0:T(8,128)} %bitcast.18, f32[3,4,8,128]{3,2,1,0:T(8,128)} %bitcast.15, f32[3,4,8,128]{3,2,1,0:T(8,128)} %bitcast.16, f32[3,4,8,128]{3,2,1,0:T(8,128)} %bitcast.17, ...), custom_call_target="tpu_custom_call" | custom-call | tf_op jit(solution)/shard_map/pallas_call | solution.py:766
  98.2 1.5 %shard_map.122 = (f32[3,4,8,128]{3,2,1,0:T(8,128)}, f32[3,4,8,128]{3,2,1,0:T(8,128)}, f32[3,4,8,128]{3,2,1,0:T(8,128)}) custom-call(f32[3,4,8,128]{3,2,1,0:T(8,128)} %get-tuple-element.9.u, f32[3,4,8,128]{3,2,1,0:T(8,128)} %get-tuple-element.10.h, f32[3,4,8,128]{3,2,1,0:T(8,128)} %get-tuple-element.11.a), custom_call_target="tpu_custom_call" | custom-call | tf_op jit(solution)/shard_map/pallas_call | solution.py:849
